TPU v7x, 32 devices: a whole 2x2x4 slice. The times are simulated.
32 devices in a mesh: section: 2 (over y), dp: 4 (over z), tensor: 4 (over x, core).
Axes of the slice: x: 2, y: 2, z: 4, core: 2. Of those that a mesh axis runs over, the one named last changes fastest.
Arguments:
- inputs: bfloat16 [2, 1536, 2048], P(None, ('dp', 'tensor')), may hold values from -6 to 6
- cotangent: bfloat16 [2, 1536, 2048], P(None, ('dp', 'tensor')), may hold values from -6 to 6
- attn_gain: bfloat16 [2, 2048], P('section', 'dp'), may hold values from 0.25 to 1.75
- mlp_gain: bfloat16 [2, 2048], P('section', 'dp'), may hold values from 0.25 to 1.75
- w_query: bfloat16 [2, 2048, 2048], P('section', 'dp', 'tensor'), may hold values from -0.125 to 0.125
- key_weight: bfloat16 [2, 2048, 512], P('section', 'dp', 'tensor'), may hold values from -0.125 to 0.125
- value_weight: bfloat16 [2, 2048, 512], P('section', 'dp', 'tensor'), may hold values from -0.125 to 0.125
- w_output: bfloat16 [2, 2048, 2048], P('section', 'dp', 'tensor'), may hold values from -2 to 2
- w_gate: bfloat16 [2, 2048, 8192], P('section', 'dp', 'tensor'), may hold values from -0.125 to 0.125
- w_up: bfloat16 [2, 2048, 8192], P('section', 'dp', 'tensor'), may hold values from -0.125 to 0.125
- w_down: bfloat16 [2, 2048, 8192], P('section', 'dp', 'tensor'), may hold values from -0.0625 to 0.0625
Outputs:
- section_out: bfloat16 [2, 2, 1536, 2048], P('section', None, ('dp', 'tensor'))
- section_in_grad: bfloat16 [2, 2, 1536, 2048], P('section', None, ('dp', 'tensor'))
- grad_attn_gain: float32 [2, 2048], P('section', 'dp')
- grad_mlp_gain: float32 [2, 2048], P('section', 'dp')
- grad_query: float32 [2, 2048, 2048], P('section', 'dp', 'tensor')
- grad_key: float32 [2, 2048, 512], P('section', 'dp', 'tensor')
- grad_value: float32 [2, 2048, 512], P('section', 'dp', 'tensor')
- grad_output: float32 [2, 2048, 2048], P('section', 'dp', 'tensor')
- grad_gate: float32 [2, 2048, 8192], P('section', 'dp', 'tensor')
- grad_up: float32 [2, 2048, 8192], P('section', 'dp', 'tensor')
- grad_down: float32 [2, 2048, 8192], P('section', 'dp', 'tensor')
All inputs are finite; a program needn't handle non-finite values.
Results may differ from a plain program's by a relative error of at most 0.034.
Values may be sent and summed in bfloat16 or wider, within the bound.
No kernel may reach another device: no remote copies, remote signals or barrier semaphores. Data moves between devices by JAX's collectives and lax.ppermute only.
A program may use at most 256 MiB of HBM per device.

v0:
```python
import jax
import jax.numpy as jnp
from jax import lax
from jax.sharding import PartitionSpec as P

HEAD_WIDTH = 64


norm_eps = 1e-05
rope_base = 500000.0


def passed_along(shard, axis, by):
    length = lax.axis_size(axis)
    pairs = [(i, i + by) for i in range(length) if 0 <= i + by < length]
    return lax.ppermute(shard, axis, pairs)


def for_sending(shard):
    return jax.tree.map(lambda a: a.astype(jnp.bfloat16) if a.dtype == jnp.float32 else a, shard)


def rope_tables(token_length, head_size):
    half = head_size // 2
    frequency = rope_base ** (-(jnp.arange(half, dtype=jnp.float32) * 2.0 / head_size))
    angles = jnp.arange(token_length, dtype=jnp.float32)[:, None] * frequency[None, :]
    return (jnp.cos(angles), jnp.sin(angles))


def rotate(values, cosine, sine, direction):
    half = values.shape[-1] // 2
    cos_part = cosine[:, None, :]
    sin_part = sine[:, None, :] * direction
    first = values[..., :half]
    second = values[..., half:]
    return jnp.concatenate(
        [first * cos_part - second * sin_part, second * cos_part + first * sin_part], axis=-1
    )


def product(left, right):
    return jnp.dot(left, right, preferred_element_type=jnp.float32)


def contract_last(left, right):
    return lax.dot_general(
        left, right, (((1,), (1,)), ((), ())), preferred_element_type=jnp.float32
    )


def contract_first(left, right):
    return lax.dot_general(
        left, right, (((0,), (0,)), ((), ())), preferred_element_type=jnp.float32
    )


def normalize(rows):
    inverse = lax.rsqrt(jnp.mean(rows * rows, axis=-1, keepdims=True) + norm_eps)
    return (rows * inverse, inverse)


def norm_back(grad_normed, unit, inverse, gain):
    scaled = grad_normed * gain
    return inverse * (scaled - unit * jnp.mean(scaled * unit, axis=-1, keepdims=True))


def split_blocks(token_length):
    return (token_length, token_length // token_length)


def masked_scores(query_block, key_rows, start):
    block_rows = query_block.shape[0]
    token_length = key_rows.shape[0]
    scores = jnp.einsum(
        "qkgd,Kkd->kgqK", query_block, key_rows, preferred_element_type=jnp.float32
    ) * HEAD_WIDTH ** (-0.5)
    causal = (start + jnp.arange(block_rows))[:, None] >= jnp.arange(token_length)[None, :]
    return jnp.where(causal, scores, -1e30)


def attend_forward(queries, key_rows, value_row_block):
    token_length, heads, width = queries.shape
    shared = key_rows.shape[1]
    block_rows, tally_count = split_blocks(token_length)
    grouped = queries.reshape(tally_count, block_rows, shared, heads // shared, width)
    starts = jnp.arange(tally_count, dtype=jnp.int32) * block_rows

    def one_block(pair):
        query_block, start = pair
        scores = masked_scores(query_block, key_rows, start)
        top = jnp.max(scores, axis=-1, keepdims=True)
        log_total = top + jnp.log(jnp.sum(jnp.exp(scores - top), axis=-1, keepdims=True))
        probs = jnp.exp(scores - log_total).astype(jnp.bfloat16)
        mixed = jnp.einsum(
            "kgqK,Kkd->qkgd", probs, value_row_block, preferred_element_type=jnp.float32
        )
        return (mixed.astype(jnp.bfloat16), log_total)

    mixed, log_total = lax.map(one_block, (grouped, starts))
    return (mixed.reshape(token_length, heads * width), log_total)


def attend_backward(queries, key_rows, value_row_block, log_total, grad_mixed):
    token_length, heads, width = queries.shape
    shared = key_rows.shape[1]
    block_rows, tally_count = split_blocks(token_length)
    shape = (tally_count, block_rows, shared, heads // shared, width)
    starts = jnp.arange(tally_count, dtype=jnp.int32) * block_rows
    scale = HEAD_WIDTH ** (-0.5)

    def one_block(carry, parts):
        key_sum, value_sum = carry
        query_block, block_total, grad_block, start = parts
        scores = masked_scores(query_block, key_rows, start)
        probs = jnp.exp(scores - block_total)
        grad_probs = jnp.einsum(
            "qkgd,Kkd->kgqK", grad_block, value_row_block, preferred_element_type=jnp.float32
        )
        delta = jnp.sum(grad_probs * probs, axis=-1, keepdims=True)
        grad_scores = (probs * (grad_probs - delta)).astype(jnp.bfloat16)
        grad_block_queries = (
            jnp.einsum("kgqK,Kkd->qkgd", grad_scores, key_rows, preferred_element_type=jnp.float32)
            * scale
        )
        key_sum = (
            key_sum
            + jnp.einsum(
                "kgqK,qkgd->Kkd", grad_scores, query_block, preferred_element_type=jnp.float32
            )
            * scale
        )
        value_sum = value_sum + jnp.einsum(
            "kgqK,qkgd->Kkd",
            probs.astype(jnp.bfloat16),
            grad_block,
            preferred_element_type=jnp.float32,
        )
        return ((key_sum, value_sum), grad_block_queries)

    zeros = jnp.zeros(key_rows.shape, jnp.float32)
    sums, grad_queries = lax.scan(
        one_block,
        (zeros, zeros),
        (queries.reshape(shape), log_total, grad_mixed.reshape(shape), starts),
    )
    return (grad_queries.reshape(token_length, heads, width), sums[0], sums[1])


def forward_block(start, weights):
    w_query, key_weight, value_weight, w_output, w_gate, w_up, w_down, attn_gain, mlp_gain = weights
    unit_a, inverse_a = normalize(start)
    first_normalized = (unit_a * attn_gain).astype(jnp.bfloat16)
    rows_a = lax.all_gather(first_normalized, "tensor", axis=0, tiled=True)
    token_length = rows_a.shape[0]
    cosine, sine = rope_tables(token_length, HEAD_WIDTH)
    query_proj = product(rows_a, w_query).reshape(token_length, -1, HEAD_WIDTH)
    key_projected = product(rows_a, key_weight).reshape(token_length, -1, HEAD_WIDTH)
    queries = rotate(query_proj, cosine, sine, 1.0).astype(jnp.bfloat16)
    key_rows = rotate(key_projected, cosine, sine, 1.0).astype(jnp.bfloat16)
    value_row_block = (
        product(rows_a, value_weight).astype(jnp.bfloat16).reshape(token_length, -1, HEAD_WIDTH)
    )
    mixed, log_total = attend_forward(queries, key_rows, value_row_block)
    attn_branch = lax.psum_scatter(
        contract_last(mixed, w_output).astype(jnp.bfloat16),
        "tensor",
        scatter_dimension=0,
        tiled=True,
    ).astype(jnp.float32)
    middle = start + attn_branch
    unit_b, inverse_b = normalize(middle)
    normed_b = (unit_b * mlp_gain).astype(jnp.bfloat16)
    rows_b = lax.all_gather(normed_b, "tensor", axis=0, tiled=True)
    gate = product(rows_b, w_gate)
    up_proj = product(rows_b, w_up)
    hidden = (jax.nn.silu(gate) * up_proj).astype(jnp.bfloat16)
    mlp_branch = lax.psum_scatter(
        contract_last(hidden, w_down).astype(jnp.bfloat16),
        "tensor",
        scatter_dimension=0,
        tiled=True,
    ).astype(jnp.float32)
    result = middle + mlp_branch
    kept = (
        unit_a,
        inverse_a,
        rows_a,
        queries,
        key_rows,
        value_row_block,
        mixed,
        log_total,
        unit_b,
        inverse_b,
        rows_b,
        gate,
        up_proj,
        hidden,
    )
    return (result, kept)


def backward_block(grad_out, kept, weights):
    w_query, key_weight, value_weight, w_output, w_gate, w_up, w_down, attn_gain, mlp_gain = weights
    (
        unit_a,
        inverse_a,
        rows_a,
        queries,
        key_rows,
        value_row_block,
        mixed,
        log_total,
        unit_b,
        inverse_b,
        rows_b,
        gate,
        up_proj,
        hidden,
    ) = kept
    out_rows = lax.all_gather(grad_out.astype(jnp.bfloat16), "tensor", axis=0, tiled=True)
    grad_wdown = contract_first(out_rows, hidden)
    grad_hidden = product(out_rows, w_down)
    sigmoid = jax.nn.sigmoid(gate)
    grad_gate = (grad_hidden * up_proj * sigmoid * (1.0 + gate * (1.0 - sigmoid))).astype(
        jnp.bfloat16
    )
    grad_upper = (grad_hidden * gate * sigmoid).astype(jnp.bfloat16)
    grad_wgate = contract_first(rows_b, grad_gate)
    grad_wup = contract_first(rows_b, grad_upper)
    part_b = contract_last(grad_gate, w_gate) + contract_last(grad_upper, w_up)
    grad_normed_b = lax.psum_scatter(
        part_b.astype(jnp.bfloat16), "tensor", scatter_dimension=0, tiled=True
    ).astype(jnp.float32)
    gain_b = jnp.sum(grad_normed_b * unit_b, axis=0)
    grad_middle = grad_out + norm_back(grad_normed_b, unit_b, inverse_b, mlp_gain)
    branch_rows = lax.all_gather(grad_middle.astype(jnp.bfloat16), "tensor", axis=0, tiled=True)
    grad_woutput = contract_first(branch_rows, mixed)
    grad_mixed = product(branch_rows, w_output).astype(jnp.bfloat16)
    grad_queries, grad_keys, grad_values = attend_backward(
        queries, key_rows, value_row_block, log_total, grad_mixed
    )
    token_length = rows_a.shape[0]
    cosine, sine = rope_tables(token_length, HEAD_WIDTH)
    grad_query_proj = (
        rotate(grad_queries, cosine, sine, -1.0).astype(jnp.bfloat16).reshape(token_length, -1)
    )
    grad_key_proj = (
        rotate(grad_keys, cosine, sine, -1.0).astype(jnp.bfloat16).reshape(token_length, -1)
    )
    grad_value_proj = grad_values.astype(jnp.bfloat16).reshape(token_length, -1)
    grad_wquery = contract_first(rows_a, grad_query_proj)
    grad_wkey = contract_first(rows_a, grad_key_proj)
    grad_wvalue = contract_first(rows_a, grad_value_proj)
    part_a = (
        contract_last(grad_query_proj, w_query)
        + contract_last(grad_key_proj, key_weight)
        + contract_last(grad_value_proj, value_weight)
    )
    grad_normed_a = lax.psum_scatter(
        part_a.astype(jnp.bfloat16), "tensor", scatter_dimension=0, tiled=True
    ).astype(jnp.float32)
    gain_a = jnp.sum(grad_normed_a * unit_a, axis=0)
    grad_start = grad_middle + norm_back(grad_normed_a, unit_a, inverse_a, attn_gain)
    matrix_grads = (
        grad_wquery,
        grad_wkey,
        grad_wvalue,
        grad_woutput,
        grad_wgate,
        grad_wup,
        grad_wdown,
    )
    return (grad_start, matrix_grads, (gain_a, gain_b))


def per_device(
    inputs,
    cotangent,
    attn_gain,
    mlp_gain,
    w_query,
    key_weight,
    value_weight,
    w_output,
    w_gate,
    w_up,
    w_down,
):
    gathered = (
        lax.all_gather(w_query, "dp", axis=1, tiled=True),
        lax.all_gather(key_weight, "dp", axis=1, tiled=True),
        lax.all_gather(value_weight, "dp", axis=1, tiled=True),
        lax.all_gather(w_output, "dp", axis=1, tiled=True),
        lax.all_gather(w_gate, "dp", axis=1, tiled=True),
        lax.all_gather(w_up, "dp", axis=1, tiled=True),
        lax.all_gather(w_down, "dp", axis=1, tiled=True),
        lax.all_gather(attn_gain, "dp", axis=1, tiled=True),
        lax.all_gather(mlp_gain, "dp", axis=1, tiled=True),
    )
    weights = tuple((piece[0] for piece in gathered))
    first_section = lax.axis_index("section") == 0
    micro = inputs.shape[0]
    empty = jnp.zeros_like(inputs[0])
    received = empty
    results = []
    kept_states = []
    for tick in range(micro + 1):
        own = inputs[tick] if tick < micro else empty
        start = jnp.where(first_section, own, received).astype(jnp.float32)
        result, kept = forward_block(start, weights)
        sent = result.astype(jnp.bfloat16)
        results.append(sent)
        kept_states.append(kept)
        if tick < micro:
            received = passed_along(sent, "section", 1)
    back_received = empty
    totals = None
    gain_total = None
    input_grads = []
    for tick in range(micro + 1):
        own = cotangent[micro - 1 - tick] if tick < micro else empty
        incoming = jnp.where(first_section, back_received, own).astype(jnp.float32)
        grad_start, matrix_grads, gain_grads = backward_block(
            incoming, kept_states[micro - tick], weights
        )
        totals = matrix_grads if totals is None else jax.tree.map(jnp.add, totals, matrix_grads)
        gain_total = (
            gain_grads if gain_total is None else jax.tree.map(jnp.add, gain_total, gain_grads)
        )
        sent = grad_start.astype(jnp.bfloat16)
        input_grads.append(sent)
        if tick < micro:
            back_received = passed_along(sent, "section", -1)
    totals = jax.tree.map(
        lambda part: part.astype(jnp.float32),
        lax.psum_scatter(for_sending(totals), "dp", scatter_dimension=0, tiled=True),
    )
    gain_full = lax.psum(gain_total, ("dp", "tensor"))
    piece = attn_gain.shape[1]
    offset = lax.axis_index("dp") * piece
    grad_attn = lax.dynamic_slice_in_dim(gain_full[0], offset, piece)[None]
    grad_mlp = lax.dynamic_slice_in_dim(gain_full[1], offset, piece)[None]
    section_out = jnp.stack(
        [jnp.where(first_section, results[index], results[index + 1]) for index in range(micro)]
    )[None]
    section_in_grad = jnp.stack(
        [
            jnp.where(first_section, input_grads[micro - index], input_grads[micro - 1 - index])
            for index in range(micro)
        ]
    )[None]
    return (section_out, section_in_grad, grad_attn, grad_mlp) + tuple(
        (total[None] for total in totals)
    )


def solution(mesh):
    placed = (
        P(None, ("dp", "tensor"), None),
        P(None, ("dp", "tensor"), None),
        P("section", "dp"),
        P("section", "dp"),
        P("section", "dp", "tensor"),
        P("section", "dp", "tensor"),
        P("section", "dp", "tensor"),
        P("section", "dp", "tensor"),
        P("section", "dp", "tensor"),
        P("section", "dp", "tensor"),
        P("section", "dp", "tensor"),
    )
    return jax.shard_map(
        per_device,
        mesh=mesh,
        in_specs=placed,
        out_specs=(
            P("section", None, ("dp", "tensor"), None),
            P("section", None, ("dp", "tensor"), None),
            P("section", "dp"),
            P("section", "dp"),
            P("section", "dp", "tensor"),
            P("section", "dp", "tensor"),
            P("section", "dp", "tensor"),
            P("section", "dp", "tensor"),
            P("section", "dp", "tensor"),
            P("section", "dp", "tensor"),
            P("section", "dp", "tensor"),
        ),
        check_vma=False,
    )
```

profile of v0, /device:TPU:0, one launch (start us, length us, event | category | flops | bytes accessed | tf_op | source)
XLA Modules:
  0.0 2008.6 jit_solution(17946694165482379620)
XLA Ops:
  26.2 16.7 all_gather.65
  42.9 15.3 all_gather.66
  64.9 27.5 %all-gather.21.cloned.1.call-done = bf16[1,2048,512]{2,1,0:T(8,128)(2,1)} async-done(((bf16[1,512,512]{2,1,0:T(8,128)(2,1)}), bf16[1,2048,512]{2,1,0:T(8,128)(2,1)}) %all-gather.21.cloned.1.call-update) | async-done | bytes 2097168 | tf_op jit(solution)/shard_map/all_gather | solution.py:291
  103.9 34.6 %all-gather.23.cloned.1.call-done = bf16[1,2048,512]{2,1,0:T(8,128)(2,1)} async-done(((bf16[1,512,512]{2,1,0:T(8,128)(2,1)}), bf16[1,2048,512]{2,1,0:T(8,128)(2,1)}) %all-gather.23.cloned.1.call-update) | async-done | bytes 2097168 | tf_op jit(solution)/shard_map/all_gather | solution.py:294
  175.0 17.5 all-gather.25.cloned.1.call-done
  192.5 151.2 %all-gather.27.cloned.1.call-done = bf16[1,2048,2048]{2,1,0:T(8,128)(2,1)} async-done(((bf16[1,512,2048]{2,1,0:T(8,128)(2,1)}), bf16[1,2048,2048]{2,1,0:T(8,128)(2,1)}) %all-gather.27.cloned.1.call-update) | async-done | bytes 8388624 | tf_op jit(solution)/shard_map/all_gather | solution.py:295
  352.6 140.6 %all-gather.29.cloned.1.call-done = bf16[1,2048,2048]{2,1,0:T(8,128)(2,1)} async-done(((bf16[1,512,2048]{2,1,0:T(8,128)(2,1)}), bf16[1,2048,2048]{2,1,0:T(8,128)(2,1)}) %all-gather.29.cloned.1.call-update) | async-done | bytes 8388624 | tf_op jit(solution)/shard_map/all_gather | solution.py:296
  503.8 138.9 %all-gather.31.cloned.1.call-done = bf16[1,2048,2048]{2,1,0:T(8,128)(2,1)} async-done(((bf16[1,512,2048]{2,1,0:T(8,128)(2,1)}), bf16[1,2048,2048]{2,1,0:T(8,128)(2,1)}) %all-gather.31.cloned.1.call-update) | async-done | bytes 8388624 | tf_op jit(solution)/shard_map/all_gather | solution.py:297
  651.3 26.5 %reduce-scatter.22.cloned.1.call-done = bf16[96,2048]{1,0:T(8,128)(2,1)} async-done(((bf16[384,2048]{1,0:T(8,128)(2,1)}), bf16[96,2048]{1,0:T(8,128)(2,1)}) %reduce-scatter.22.cloned.1.call-update) | async-done | bytes 393232 | tf_op jit(solution)/shard_map/reduce_scatter | solution.py:177
  692.3 20.5 %all-gather.33.cloned.1.call-done = bf16[384,2048]{1,0:T(8,128)(2,1)} async-done(((bf16[96,2048]{1,0:T(8,128)(2,1)}), bf16[384,2048]{1,0:T(8,128)(2,1)}) %all-gather.33.cloned.1.call-update) | async-done | bytes 1572880 | tf_op jit(solution)/shard_map/all_gather | solution.py:153
  724.0 28.3 %reduce-scatter.24.cloned.1.call-done = bf16[96,2048]{1,0:T(8,128)(2,1)} async-done(((bf16[384,2048]{1,0:T(8,128)(2,1)}), bf16[96,2048]{1,0:T(8,128)(2,1)}) %reduce-scatter.24.cloned.1.call-update) | async-done | bytes 393232 | tf_op jit(solution)/shard_map/reduce_scatter | solution.py:164
  756.0 19.3 all-gather.35.cloned.1.call-done
  798.4 28.3 %reduce-scatter.26.cloned.1.call-done = bf16[96,2048]{1,0:T(8,128)(2,1)} async-done(((bf16[384,2048]{1,0:T(8,128)(2,1)}), bf16[96,2048]{1,0:T(8,128)(2,1)}) %reduce-scatter.26.cloned.1.call-update) | async-done | bytes 393232 | tf_op jit(solution)/shard_map/reduce_scatter | solution.py:177
  841.8 20.6 %all-gather.37.cloned.1.call-done = bf16[384,2048]{1,0:T(8,128)(2,1)} async-done(((bf16[96,2048]{1,0:T(8,128)(2,1)}), bf16[384,2048]{1,0:T(8,128)(2,1)}) %all-gather.37.cloned.1.call-update) | async-done | bytes 1572880 | tf_op jit(solution)/shard_map/all_gather | solution.py:153
  874.5 27.4 %reduce-scatter.28.cloned.1.call-done = bf16[96,2048]{1,0:T(8,128)(2,1)} async-done(((bf16[384,2048]{1,0:T(8,128)(2,1)}), bf16[96,2048]{1,0:T(8,128)(2,1)}) %reduce-scatter.28.cloned.1.call-update) | async-done | bytes 393232 | tf_op jit(solution)/shard_map/reduce_scatter | solution.py:164
  905.4 18.3 all-gather.51.cloned.1.call-done
  973.4 28.3 %reduce-scatter.32.cloned.1.call-done = bf16[96,2048]{1,0:T(8,128)(2,1)} async-done(((bf16[384,2048]{1,0:T(8,128)(2,1)}), bf16[96,2048]{1,0:T(8,128)(2,1)}) %reduce-scatter.32.cloned.1.call-update) | async-done | bytes 393232 | tf_op jit(solution)/shard_map/reduce_scatter | solution.py:232
  1006.0 19.5 all-gather.41.cloned.1.call-done
  1043.8 28.3 %reduce-scatter.34.cloned.1.call-done = bf16[96,2048]{1,0:T(8,128)(2,1)} async-done(((bf16[384,2048]{1,0:T(8,128)(2,1)}), bf16[96,2048]{1,0:T(8,128)(2,1)}) %reduce-scatter.34.cloned.1.call-update) | async-done | bytes 393232 | tf_op jit(solution)/shard_map/reduce_scatter | solution.py:260
  1090.8 18.4 all-gather.43.cloned.1.call-done
  1136.3 28.3 %reduce-scatter.36.cloned.1.call-done = bf16[96,2048]{1,0:T(8,128)(2,1)} async-done(((bf16[384,2048]{1,0:T(8,128)(2,1)}), bf16[96,2048]{1,0:T(8,128)(2,1)}) %reduce-scatter.36.cloned.1.call-update) | async-done | bytes 393232 | tf_op jit(solution)/shard_map/reduce_scatter | solution.py:232
  1169.4 19.6 all-gather.45.cloned.1.call-done
  1209.7 28.3 %reduce-scatter.38.cloned.1.call-done = bf16[96,2048]{1,0:T(8,128)(2,1)} async-done(((bf16[384,2048]{1,0:T(8,128)(2,1)}), bf16[96,2048]{1,0:T(8,128)(2,1)}) %reduce-scatter.38.cloned.1.call-update) | async-done | bytes 393232 | tf_op jit(solution)/shard_map/reduce_scatter | solution.py:260
  1256.4 18.6 all-gather.47.cloned.1.call-done
  1302.2 28.3 %reduce-scatter.40.cloned.1.call-done = bf16[96,2048]{1,0:T(8,128)(2,1)} async-done(((bf16[384,2048]{1,0:T(8,128)(2,1)}), bf16[96,2048]{1,0:T(8,128)(2,1)}) %reduce-scatter.40.cloned.1.call-update) | async-done | bytes 393232 | tf_op jit(solution)/shard_map/reduce_scatter | solution.py:232
  1419.7 19.6 add_convert_fusion.2
  1457.7 17.0 add_convert_fusion.1
  1494.2 17.1 add_convert_fusion
  1519.6 63.4 %all-reduce = (f32[2048]{0:T(1024)S(1)}, f32[2048]{0:T(1024)S(1)}) all-reduce(f32[2048]{0:T(1024)S(1)} %add_add_fusion.1, f32[2048]{0:T(1024)S(1)} %add_add_fusion), channel_id=1, replica_groups=mesh['section'=2,'dp'=4,'tensor'=4] {'dp','tensor'}, use_global_device_ids=true, to_apply=%region_36.37 | all-reduce | flops 4096 | bytes 32768 | tf_op jit(solution)/shard_map/psum | solution.py:339
  1591.2 111.1 %reduce-scatter.52.cloned.1.call-done = bf16[512,2048]{1,0:T(8,128)(2,1)} async-done(((bf16[2048,2048]{1,0:T(8,128)(2,1)}), bf16[512,2048]{1,0:T(8,128)(2,1)}) %reduce-scatter.52.cloned.1.call-update) | async-done | bytes 2097168 | tf_op jit(solution)/shard_map/reduce_scatter | solution.py:337
  1706.4 143.5 %reduce-scatter.54.cloned.1.call-done = bf16[512,2048]{1,0:T(8,128)(2,1)} async-done(((bf16[2048,2048]{1,0:T(8,128)(2,1)}), bf16[512,2048]{1,0:T(8,128)(2,1)}) %reduce-scatter.54.cloned.1.call-update) | async-done | bytes 2097168 | tf_op jit(solution)/shard_map/reduce_scatter | solution.py:337
  1854.1 143.3 %reduce-scatter.56.cloned.1.call-done = bf16[512,2048]{1,0:T(8,128)(2,1)} async-done(((bf16[2048,2048]{1,0:T(8,128)(2,1)}), bf16[512,2048]{1,0:T(8,128)(2,1)}) %reduce-scatter.56.cloned.1.call-update) | async-done | bytes 2097168 | tf_op jit(solution)/shard_map/reduce_scatter | solution.py:337
  (587 shorter events, 527.4 us)
Async XLA Ops:
  24.7 67.7 %all-gather.21.cloned.1.call-start = ((), (), s32[]{:S(2)}) async-start(), calls=%async_computation.20 | async-start | bytes 2621440 | tf_op jit(solution)/shard_map/all_gather | solution.py:291
  25.4 113.1 %all-gather.23.cloned.1.call-start = ((), (), s32[]{:S(2)}) async-start(), calls=%async_computation.21 | async-start | bytes 2621440 | tf_op jit(solution)/shard_map/all_gather | solution.py:294
  26.1 143.3 %reduce-scatter.20.cloned.1.call-start = ((), (), s32[]{:S(2)}) async-start(), calls=%async_computation.22 | async-start | bytes 1966080 | tf_op jit(solution)/shard_map/reduce_scatter | solution.py:164
  172.7 171.0 %all-gather.27.cloned.1.call-start = ((), (), s32[]{:S(2)}) async-start(), calls=%async_computation.24 | async-start | bytes 10485760 | tf_op jit(solution)/shard_map/all_gather | solution.py:295
  173.2 320.0 %all-gather.29.cloned.1.call-start = ((), (), s32[]{:S(2)}) async-start(), calls=%async_computation.25 | async-start | bytes 10485760 | tf_op jit(solution)/shard_map/all_gather | solution.py:296
  174.0 468.8 %all-gather.31.cloned.1.call-start = ((), (), s32[]{:S(2)}) async-start(), calls=%async_computation.26 | async-start | bytes 10485760 | tf_op jit(solution)/shard_map/all_gather | solution.py:297
  174.7 503.1 %reduce-scatter.22.cloned.1.call-start = ((), (), s32[]{:S(2)}) async-start(), calls=%async_computation.27 | async-start | bytes 1966080 | tf_op jit(solution)/shard_map/reduce_scatter | solution.py:177
  651.3 61.5 %all-gather.33.cloned.1.call-start = ((), (), s32[]{:S(2)}) async-start(), calls=%async_computation.28 | async-start | bytes 1966080 | tf_op jit(solution)/shard_map/all_gather | solution.py:153
  692.0 60.3 %reduce-scatter.24.cloned.1.call-start = ((), (), s32[]{:S(2)}) async-start(), calls=%async_computation.29 | async-start | bytes 1966080 | tf_op jit(solution)/shard_map/reduce_scatter | solution.py:164
  755.5 71.2 %reduce-scatter.26.cloned.1.call-start = ((), (), s32[]{:S(2)}) async-start(), calls=%async_computation.31 | async-start | bytes 1966080 | tf_op jit(solution)/shard_map/reduce_scatter | solution.py:177
  798.4 64.1 %all-gather.37.cloned.1.call-start = ((), (), s32[]{:S(2)}) async-start(), calls=%async_computation.32 | async-start | bytes 1966080 | tf_op jit(solution)/shard_map/all_gather | solution.py:153
  841.6 60.3 %reduce-scatter.28.cloned.1.call-start = ((), (), s32[]{:S(2)}) async-start(), calls=%async_computation.33 | async-start | bytes 1966080 | tf_op jit(solution)/shard_map/reduce_scatter | solution.py:164
  874.4 71.0 %all-gather.39.cloned.1.call-start = ((), (), s32[]{:S(2)}) async-start(), calls=%async_computation.34 | async-start | bytes 1966080 | tf_op jit(solution)/shard_map/all_gather | solution.py:173
  905.1 96.5 %reduce-scatter.32.cloned.1.call-start = ((), (), s32[]{:S(2)}) async-start(), calls=%async_computation.36 | async-start | bytes 1966080 | tf_op jit(solution)/shard_map/reduce_scatter | solution.py:232
  973.3 52.2 %all-gather.41.cloned.1.call-start = ((), (), s32[]{:S(2)}) async-start(), calls=%async_computation.37 | async-start | bytes 1966080 | tf_op jit(solution)/shard_map/all_gather | solution.py:237
  1005.7 66.4 %reduce-scatter.34.cloned.1.call-start = ((), (), s32[]{:S(2)}) async-start(), calls=%async_computation.38 | async-start | bytes 1966080 | tf_op jit(solution)/shard_map/reduce_scatter | solution.py:260
  1043.7 65.5 %all-gather.43.cloned.1.call-start = ((), (), s32[]{:S(2)}) async-start(), calls=%async_computation.39 | async-start | bytes 1966080 | tf_op jit(solution)/shard_map/all_gather | solution.py:221
  1090.3 74.2 %reduce-scatter.36.cloned.1.call-start = ((), (), s32[]{:S(2)}) async-start(), calls=%async_computation.40 | async-start | bytes 1966080 | tf_op jit(solution)/shard_map/reduce_scatter | solution.py:232
  1136.2 52.8 %all-gather.45.cloned.1.call-start = ((), (), s32[]{:S(2)}) async-start(), calls=%async_computation.41 | async-start | bytes 1966080 | tf_op jit(solution)/shard_map/all_gather | solution.py:237
  1169.2 68.8 %reduce-scatter.38.cloned.1.call-start = ((), (), s32[]{:S(2)}) async-start(), calls=%async_computation.42 | async-start | bytes 1966080 | tf_op jit(solution)/shard_map/reduce_scatter | solution.py:260
  1209.7 65.4 %all-gather.47.cloned.1.call-start = ((), (), s32[]{:S(2)}) async-start(), calls=%async_computation.43 | async-start | bytes 1966080 | tf_op jit(solution)/shard_map/all_gather | solution.py:221
  1256.1 74.4 %reduce-scatter.40.cloned.1.call-start = ((), (), s32[]{:S(2)}) async-start(), calls=%async_computation.44 | async-start | bytes 1966080 | tf_op jit(solution)/shard_map/reduce_scatter | solution.py:232
  1302.2 53.0 %all-gather.49.cloned.1.call-start = ((), (), s32[]{:S(2)}) async-start(), calls=%async_computation.45 | async-start | bytes 1966080 | tf_op jit(solution)/shard_map/all_gather | solution.py:237
  1335.4 176.0 %reduce-scatter.30.cloned.1.call-start = ((), (), s32[]{:S(2)}) async-start(), calls=%async_computation.35 | async-start | bytes 1966080 | tf_op jit(solution)/shard_map/reduce_scatter | solution.py:177
  1344.0 170.9 %reduce-scatter.46.cloned.1.call-start = ((), (), s32[]{:S(2)}) async-start(), calls=%async_computation.48 | async-start | bytes 655360 | tf_op jit(solution)/shard_map/reduce_scatter | solution.py:337
  1370.1 146.4 %reduce-scatter.48.cloned.1.call-start = ((), (), s32[]{:S(2)}) async-start(), calls=%async_computation.49 | async-start | bytes 655360 | tf_op jit(solution)/shard_map/reduce_scatter | solution.py:337
  1381.0 137.2 %reduce-scatter.42.cloned.1.call-start = ((), (), s32[]{:S(2)}) async-start(), calls=%async_computation.46 | async-start | bytes 1966080 | tf_op jit(solution)/shard_map/reduce_scatter | solution.py:260
  1385.5 201.4 %reduce-scatter.44.cloned.1.call-start = ((), (), s32[]{:S(2)}) async-start(), calls=%async_computation.47 | async-start | bytes 2621440 | tf_op jit(solution)/shard_map/reduce_scatter | solution.py:337
  1392.4 196.6 %reduce-scatter.50.cloned.1.call-start = ((), (), s32[]{:S(2)}) async-start(), calls=%async_computation.50 | async-start | bytes 2621440 | tf_op jit(solution)/shard_map/reduce_scatter | solution.py:337
  1400.2 302.1 %reduce-scatter.52.cloned.1.call-start = ((), (), s32[]{:S(2)}) async-start(), calls=%async_computation.51 | async-start | bytes 10485760 | tf_op jit(solution)/shard_map/reduce_scatter | solution.py:337
  1439.4 410.6 %reduce-scatter.54.cloned.1.call-start = ((), (), s32[]{:S(2)}) async-start(), calls=%async_computation.52 | async-start | bytes 10485760 | tf_op jit(solution)/shard_map/reduce_scatter | solution.py:337
  1474.8 522.7 %reduce-scatter.56.cloned.1.call-start = ((), (), s32[]{:S(2)}) async-start(), calls=%async_computation.53 | async-start | bytes 10485760 | tf_op jit(solution)/shard_map/reduce_scatter | solution.py:337
  (168 other events, 4920.7 us)
Sparse Core Ops, SparseCore 0:
  45.8 46.5 all-gather.20
  94.0 44.5 all-gather.22
  142.4 26.9 reduce-scatter.19
  172.8 19.6 all-gather.24
  194.0 149.6 all-gather.26
  345.3 147.8 all-gather.28
  494.8 147.8 all-gather.30
  651.4 26.3 reduce-scatter.21
  692.1 20.6 all-gather.32
  724.1 28.1 reduce-scatter.23
  755.6 19.6 all-gather.34
  798.5 28.1 reduce-scatter.25
  841.7 20.6 all-gather.36
  873.7 28.1 reduce-scatter.27
  904.0 19.6 all-gather.50
  925.7 19.6 all-gather.38
  973.4 28.1 reduce-scatter.31
  1005.8 19.6 all-gather.40
  1043.9 28.1 reduce-scatter.33
  1136.3 28.1 reduce-scatter.35
  1169.3 19.6 all-gather.44
  1209.8 28.1 reduce-scatter.37
  1302.3 28.1 reduce-scatter.39
  1358.2 28.1 reduce-scatter.29
  1389.4 21.6 reduce-scatter.45
  1413.8 19.8 reduce-scatter.47
  1436.4 26.4 reduce-scatter.41
  1465.8 43.8 reduce-scatter.43
  1512.5 43.4 reduce-scatter.49
  1558.4 143.8 reduce-scatter.51
  1704.7 145.2 reduce-scatter.53
  1852.2 145.1 reduce-scatter.55
  (4 shorter events, 76.2 us)
where the time goes:
time: 2020 us; the launch traced here: 2010 us
  waiting for transfers between devices  1390 us (69%)
  matrix products  363 us (18%)
  blocking collectives  121 us (6%)
  other arithmetic  78.2 us (4%)
  local copies, waits for them, and re-layouts  25.4 us (1%)
    reduce_scatter x7, waiting for transfers between devices, per_device(): lax.psum_scatter(for_sending(totals), 'dp', scatter_dimension=0, tiled=True)  398 us
    all_gather x1, waiting for transfers between devices, per_device(): lax.all_gather(w_gate, 'dp', axis=1, tiled=True)  151 us
    all_gather x1, waiting for transfers between devices, per_device(): lax.all_gather(w_up, 'dp', axis=1, tiled=True)  141 us
    all_gather x1, waiting for transfers between devices, per_device(): lax.all_gather(w_down, 'dp', axis=1, tiled=True)  139 us
    dot_general x21, matrix products, contract_first(): lax.dot_general(left, right, (((0,), (0,)), ((), ())), preferred_element_...  130 us
    dot_general x21, matrix products, product(): return jnp.dot(left, right, preferred_element_type=jnp.float32)  109 us
    dot_general x21, matrix products, contract_last(): lax.dot_general(left, right, (((1,), (1,)), ((), ())), preferred_element_...  87.7 us
    reduce_scatter x3, waiting for transfers between devices, backward_block(): lax.psum_scatter(part_b.astype(jnp.bfloat16), 'tensor', scatter_dimension...  84.9 us
  transfers between devices with their start and end apart: 40, of which 33 were waited for; matrix products, arithmetic and copies ran while one was open for 12% of the time, Pallas kernels for 0%

commit v1 on v0

v1 whole, which is shorter than its diff:
```python
import jax
import jax.numpy as jnp
from jax import lax
from jax.sharding import PartitionSpec as P

HEAD_WIDTH = 64
norm_eps = 1e-05
rope_base = 500000.0
GAIN_ROWS = 16
BF16 = jnp.bfloat16
F32 = jnp.float32


def swap(shard, axis, bit):
    length = lax.axis_size(axis)
    return lax.ppermute(shard, axis, [(i, i ^ bit) for i in range(length)])


def over_core(shard):
    return swap(shard, "tensor", 1)


def over_x(shard):
    return swap(shard, "tensor", 2)


def over_y(shard):
    return swap(shard, "section", 1)


def over_z(shard):
    return swap(shard, "dp", 1)


def rows_of(parts):
    return jnp.concatenate(parts, axis=0)


def product(left, right):
    return jnp.dot(left, right, preferred_element_type=F32)


def contract_last(left, right):
    return lax.dot_general(left, right, (((1,), (1,)), ((), ())), preferred_element_type=F32)


def contract_first(left, right):
    return lax.dot_general(left, right, (((0,), (0,)), ((), ())), preferred_element_type=F32)


def gather_eight(block):
    half = block.shape[0] // 2
    by_x = over_x(block)
    by_y = over_y(block)
    by_xy = rows_of([over_x(by_y[:half]), over_y(by_x[half:])])
    own = [block, by_x, by_y, by_xy]
    peer = [over_core(part) for part in own]
    return rows_of([own[0], peer[0], own[1], peer[1], own[2], peer[2], own[3], peer[3]])


def gather_eight_replicated(blocks):
    own = blocks.shape[0]
    wide = blocks.reshape(-1, blocks.shape[2])
    by_x = over_x(wide)
    peer = over_core(wide)
    peer_x = over_core(by_x)
    cut = blocks.shape[1]
    order = []
    for micro in range(own):
        piece = slice(micro * cut, (micro + 1) * cut)
        order += [wide[piece], peer[piece], by_x[piece], peer_x[piece]]
    return rows_of(order)


def scatter_eight(parts):
    size = parts.shape[0] // 8
    half = size // 2
    block = [parts[i * size : (i + 1) * size] for i in range(8)]
    kept = []
    for own, other in ((0, 1), (2, 3), (4, 5), (6, 7)):
        kept.append(block[own].astype(F32) + over_core(block[other]).astype(F32))
    mine, to_x, to_y, to_xy = kept
    to_xy = to_xy.astype(BF16)
    from_x = over_x(to_xy[:half]).astype(F32)
    from_y = over_y(to_xy[half:]).astype(F32)
    to_y = rows_of([to_y[:half] + from_x, to_y[half:]]).astype(BF16)
    to_x = rows_of([to_x[:half], to_x[half:] + from_y]).astype(BF16)
    return mine + over_x(to_x).astype(F32) + over_y(to_y).astype(F32)


def gather_sixteen(block, by_y=None):
    by_z = over_z(block)
    by_x = over_x(block)
    if by_y is None:
        by_y = over_y(block)
    by_zx = over_x(by_z)
    by_zy = over_y(by_z)
    by_xy = over_x(by_y)
    by_zxy = over_y(by_zx)
    own = [block, by_x, by_y, by_xy, by_z, by_zx, by_zy, by_zxy]
    peer = [over_core(part) for part in own]
    return rows_of(own + peer)


def scatter_sixteen(parts):
    size = parts.shape[0] // 16
    block = [parts[i * size : (i + 1) * size] for i in range(16)]
    kept = [
        block[i].astype(F32) + over_core(block[8 + i]).astype(F32) for i in range(8)
    ]
    mine, to_x, to_y, to_xy, to_z, to_zx, to_zy, to_zxy = kept
    to_y = to_y + over_x(to_xy.astype(BF16)).astype(F32)
    to_zx = to_zx + over_y(to_zxy.astype(BF16)).astype(F32)
    to_z = (
        to_z
        + over_x(to_zx.astype(BF16)).astype(F32)
        + over_y(to_zy.astype(BF16)).astype(F32)
    )
    return (
        mine
        + over_x(to_x.astype(BF16)).astype(F32)
        + over_y(to_y.astype(BF16)).astype(F32)
        + over_z(to_z.astype(BF16)).astype(F32)
    )


def pair_groups():
    length = lax.axis_size("dp")
    return [list(range(low, length, 2)) for low in range(2)]


def ordered(low, mine, other, axis):
    return jnp.where(
        low == 0,
        jnp.concatenate([mine, other], axis=axis),
        jnp.concatenate([other, mine], axis=axis),
    )


def gather_mlp(part):
    low = lax.axis_index("dp") & 1
    half = part.shape[1] // 2
    kept = lax.dynamic_slice_in_dim(part, low * half, half, 1)
    sent = lax.dynamic_slice_in_dim(part, (1 - low) * half, half, 1)
    part = ordered(low, kept, over_z(sent), 0)
    return lax.all_gather(part, "dp", axis=0, tiled=True, axis_index_groups=pair_groups())


def reduce_mlp(grad):
    low = lax.axis_index("dp") & 1
    part = lax.psum_scatter(
        grad, "dp", scatter_dimension=0, tiled=True, axis_index_groups=pair_groups()
    )
    half = part.shape[0] // 2
    kept = lax.dynamic_slice_in_dim(part, low * half, half, 0)
    sent = lax.dynamic_slice_in_dim(part, (1 - low) * half, half, 0)
    return ordered(low, kept, over_z(sent), 1)


def normalize(rows):
    inverse = lax.rsqrt(jnp.mean(rows * rows, axis=-1, keepdims=True) + norm_eps)
    return (rows * inverse, inverse)


def norm_back(grad_normed, unit, inverse, gain):
    scaled = grad_normed * gain
    return inverse * (scaled - unit * jnp.mean(scaled * unit, axis=-1, keepdims=True))


def rotate(values, cosine, sine, direction):
    half = values.shape[-1] // 2
    cos_part = cosine[:, None, :]
    sin_part = sine[:, None, :] * direction
    first = values[..., :half]
    second = values[..., half:]
    return jnp.concatenate(
        [first * cos_part - second * sin_part, second * cos_part + first * sin_part], axis=-1
    )


def attend_forward(qkv, tables):
    cosine, sine, mask, micro = tables
    rows = qkv.shape[0]
    token_length = rows // micro
    heads = (qkv.shape[1] - 2 * HEAD_WIDTH) // HEAD_WIDTH
    width = heads * HEAD_WIDTH
    q = qkv[:, :width].reshape(micro, token_length, heads, HEAD_WIDTH)
    k = qkv[:, width : width + HEAD_WIDTH].reshape(micro, token_length, 1, HEAD_WIDTH)
    values = qkv[:, width + HEAD_WIDTH :].astype(BF16).reshape(micro, token_length, HEAD_WIDTH)
    queries = rotate(q, cosine, sine, 1.0).astype(BF16)
    keys = rotate(k, cosine, sine, 1.0).astype(BF16)[:, :, 0]
    scores = (
        jnp.einsum("sqhd,skd->sqhk", queries, keys, preferred_element_type=F32)
        * HEAD_WIDTH ** (-0.5)
    )
    scores = jnp.where(mask[None, :, None, :], scores, -1e30)
    top = jnp.max(scores, axis=-1, keepdims=True)
    exped = jnp.exp(scores - top)
    probs = exped / jnp.sum(exped, axis=-1, keepdims=True)
    mixed = jnp.einsum("sqhk,skd->sqhd", probs.astype(BF16), values, preferred_element_type=F32)
    return mixed.astype(BF16).reshape(rows, width), (queries, keys, values, probs)


def attend_backward(kept, grad_mixed, tables):
    cosine, sine, mask, micro = tables
    queries, keys, values, probs = kept
    rows, width = grad_mixed.shape
    token_length = rows // micro
    scale = HEAD_WIDTH ** (-0.5)
    grad_mixed = grad_mixed.reshape(queries.shape)
    grad_probs = jnp.einsum("sqhd,skd->sqhk", grad_mixed, values, preferred_element_type=F32)
    delta = jnp.sum(grad_probs * probs, axis=-1, keepdims=True)
    grad_scores = (probs * (grad_probs - delta)).astype(BF16)
    grad_q = jnp.einsum("sqhk,skd->sqhd", grad_scores, keys, preferred_element_type=F32) * scale
    grad_k = jnp.einsum("sqhk,sqhd->skd", grad_scores, queries, preferred_element_type=F32) * scale
    grad_v = jnp.einsum(
        "sqhk,sqhd->skd", probs.astype(BF16), grad_mixed, preferred_element_type=F32
    )
    grad_q = rotate(grad_q, cosine, sine, -1.0).astype(BF16).reshape(rows, width)
    grad_k = rotate(grad_k[:, :, None], cosine, sine, -1.0).astype(BF16).reshape(rows, HEAD_WIDTH)
    grad_v = grad_v.astype(BF16).reshape(rows, HEAD_WIDTH)
    return jnp.concatenate([grad_q, grad_k, grad_v], axis=1)


def attention_half(start, rows_a, weights, tables):
    w_qkv, w_out = weights
    mixed, kept = attend_forward(product(rows_a, w_qkv), tables)
    branch = scatter_eight(contract_last(mixed, w_out).astype(BF16))
    return start + branch, (mixed, kept)


def per_device(
    inputs,
    cotangent,
    attn_gain,
    mlp_gain,
    w_query,
    key_weight,
    value_weight,
    w_output,
    w_gate,
    w_up,
    w_down,
):
    section = lax.axis_index("section")
    place = lax.axis_index("dp")
    first = section == 0
    micro, size, features = inputs.shape
    query_cols = w_query.shape[2] // 2
    key_cols = key_weight.shape[2] // 2

    query, key, value, output = w_query[0], key_weight[0], value_weight[0], w_output[0]
    gains = jnp.stack([attn_gain[0], mlp_gain[0]])
    cut = query_cols + 2 * key_cols
    width = cut + query_cols
    depth = query.shape[0]
    gains = jnp.pad(gains, ((0, GAIN_ROWS - 2), (0, width - depth)))

    def packed(columns, key_columns):
        parts = [query[:, columns], key[:, key_columns], value[:, key_columns], output[:, columns]]
        return rows_of([jnp.concatenate(parts, axis=1), gains])

    kept = packed(slice(0, query_cols), slice(0, key_cols))
    got = over_y(packed(slice(query_cols, None), slice(key_cols, None)))
    attention = [jnp.where(first, kept, got), jnp.where(first, got, kept)]
    mlp = [[], []]
    for weight in (w_gate[0], w_up[0], w_down[0]):
        half = weight.shape[1] // 2
        got = over_y(weight[:, half:])
        mlp[0].append(jnp.where(first, weight[:, :half], got))
        mlp[1].append(jnp.where(first, got, weight[:, :half]))
    full_attention = []
    full_mlp = []
    gains = []
    for index in range(2):
        whole = lax.all_gather(attention[index], "dp", axis=0, tiled=False)
        own = whole[:, :depth].reshape(features, width)
        full_attention.append((own[:, :cut], own[:, cut:]))
        gains.append(
            [whole[:, depth + row, :depth].reshape(features).astype(F32) for row in range(2)]
        )
        full_mlp.append([gather_mlp(part) for part in mlp[index]])

    quarter = lax.axis_index("tensor")
    positions = jnp.concatenate(
        [(quarter ^ other) * size + jnp.arange(size, dtype=jnp.int32) for other in range(4)]
    )
    head_half = HEAD_WIDTH // 2
    frequency = rope_base ** (-(jnp.arange(head_half, dtype=F32) * 2.0 / HEAD_WIDTH))
    angles = positions.astype(F32)[:, None] * frequency[None, :]
    mask = positions[:, None] >= positions[None, :]
    tables = (jnp.cos(angles), jnp.sin(angles), mask, micro)

    def own_first(pair):
        return jnp.where(first, pair, jnp.stack([pair[1], pair[0]]))

    both = own_first(inputs)
    both_out = own_first(cotangent)
    start = both[0].astype(F32)
    saved = []
    outputs = []
    for index in range(2):
        if index == 0:
            unit_a, inverse_a = normalize(start)
            unit_rows, _ = normalize(gather_eight_replicated(both).astype(F32))
            rows_a = (unit_rows * gains[0][0]).astype(BF16)
        else:
            unit_a, inverse_a = normalize(start)
            rows_a = gather_eight((unit_a * gains[index][0]).astype(BF16))
        middle, (mixed, attended) = attention_half(start, rows_a, full_attention[index], tables)
        unit_b, inverse_b = normalize(middle)
        rows_b = gather_sixteen((unit_b * gains[index][1]).astype(BF16))
        gate = product(rows_b, full_mlp[index][0])
        up = product(rows_b, full_mlp[index][1])
        hidden = (jax.nn.silu(gate) * up).astype(BF16)
        branch = scatter_sixteen(contract_last(hidden, full_mlp[index][2]).astype(BF16))
        result = (middle + branch).astype(BF16)
        outputs.append(result)
        start = result.astype(F32)
        saved.append(
            (unit_a, inverse_a, rows_a, mixed, attended, unit_b, inverse_b, rows_b, gate, up, hidden)
        )

    grad = both_out[0].astype(F32)
    out_rows = gather_sixteen(both_out[0], both_out[1])
    input_grads = [None, None]
    matrix = [None, None]
    gain_grads = [None, None]
    for index in (1, 0):
        unit_a, inverse_a, rows_a, mixed, attended, unit_b, inverse_b, rows_b, gate, up, hidden = (
            saved[index]
        )
        w_qkv, w_out = full_attention[index]
        weight_gate, weight_up, weight_down = full_mlp[index]
        if index == 0:
            out_rows = gather_sixteen(grad.astype(BF16))
        grad_down = reduce_mlp(contract_first(out_rows, hidden).astype(BF16))
        grad_hidden = product(out_rows, weight_down)
        sigmoid = jax.nn.sigmoid(gate)
        grad_gate = (grad_hidden * up * sigmoid * (1.0 + gate * (1.0 - sigmoid))).astype(BF16)
        grad_up = (grad_hidden * gate * sigmoid).astype(BF16)
        normed_part = contract_last(grad_gate, weight_gate) + contract_last(grad_up, weight_up)
        grad_wgate = reduce_mlp(contract_first(rows_b, grad_gate).astype(BF16))
        grad_wup = reduce_mlp(contract_first(rows_b, grad_up).astype(BF16))
        grad_normed_b = scatter_sixteen(normed_part.astype(BF16))
        gain_b = jnp.sum(grad_normed_b * unit_b, axis=0)
        grad_middle = grad + norm_back(grad_normed_b, unit_b, inverse_b, gains[index][1])
        branch_rows = gather_eight(grad_middle.astype(BF16))
        grad_woutput = contract_first(branch_rows, mixed).astype(BF16)
        grad_mixed = product(branch_rows, w_out).astype(BF16)
        grad_qkv = attend_backward(attended, grad_mixed, tables)
        grad_wqkv = contract_first(rows_a, grad_qkv).astype(BF16)
        grad_attention = lax.psum_scatter(
            jnp.concatenate([grad_wqkv, grad_woutput], axis=1),
            "dp",
            scatter_dimension=0,
            tiled=True,
        )
        grad_normed_a = scatter_eight(contract_last(grad_qkv, w_qkv).astype(BF16))
        gain_a = jnp.sum(grad_normed_a * unit_a, axis=0)
        grad_start = grad_middle + norm_back(grad_normed_a, unit_a, inverse_a, gains[index][0])
        sent = grad_start.astype(BF16)
        input_grads[index] = sent
        grad = sent.astype(F32)
        matrix[index] = [grad_attention, grad_wgate, grad_wup, grad_down]
        gain_grads[index] = jnp.stack([gain_a, gain_b])

    whole = []
    for one, two in zip(matrix[0], matrix[1]):
        got_one = lax.ppermute(one, "section", [(1, 0)])
        got_two = lax.ppermute(two, "section", [(0, 1)])
        whole.append((jnp.where(first, one, two), jnp.where(first, got_one, got_two)))
    sizes = (query_cols, key_cols, key_cols, query_cols)
    grads = []
    offset = 0
    for width in sizes:
        grads.append(
            jnp.concatenate(
                [part[:, offset : offset + width].astype(F32) for part in whole[0]], axis=1
            )
        )
        offset += width
    for pair in whole[1:]:
        grads.append(jnp.concatenate([part.astype(F32) for part in pair], axis=1))

    gain_sum = jnp.stack(gain_grads)
    gain_sum = jnp.where(first, gain_sum[0], gain_sum[1]) + over_y(
        jnp.where(first, gain_sum[1], gain_sum[0])
    )
    bit = lax.axis_size("dp") // 2
    while bit:
        half = gain_sum.shape[1] // 2
        high = (place & bit) > 0
        low_part, high_part = gain_sum[:, :half], gain_sum[:, half:]
        gain_sum = jnp.where(high, high_part, low_part) + swap(
            jnp.where(high, low_part, high_part), "dp", bit
        )
        bit //= 2
    gain_sum = gain_sum + over_x(gain_sum)
    gain_sum = gain_sum + over_core(gain_sum)

    def by_section(one, two):
        own = jnp.where(first, one, two)
        other = over_y(jnp.where(first, two, one))
        return jnp.where(first, jnp.stack([own, other]), jnp.stack([other, own]))[None]

    return (
        by_section(outputs[0], outputs[1]),
        by_section(input_grads[0], input_grads[1]),
        gain_sum[0][None],
        gain_sum[1][None],
    ) + tuple(grad[None] for grad in grads)


def solution(mesh):
    matrix = P("section", "dp", "tensor")
    tokens = P(None, ("dp", "tensor"), None)
    gain = P("section", "dp")
    result = P("section", None, ("dp", "tensor"), None)
    return jax.shard_map(
        per_device,
        mesh=mesh,
        in_specs=(tokens, tokens, gain, gain) + (matrix,) * 7,
        out_specs=(result, result, gain, gain) + (matrix,) * 7,
        check_vma=False,
    )
```

time: 2020 us -> 1160 us (0.57)
  waiting for transfers between devices: 1390 us -> 509 us
  matrix products: 363 us -> 191 us
  starting transfers between devices: 14.6 us -> 165 us
  local copies, waits for them, and re-layouts: 25.4 us -> 162 us
  blocking collectives: 121 us -> 0 us
  other arithmetic: 78.2 us -> 114 us
    reduce_scatter x19 -> x8, waiting for transfers between devices: 665 us -> 0.01 us  [the longest x6 0.01 us: reduce_mlp(): lax.psum_scatter(grad, 'dp', scatter_dimension=0, tiled=True, axis_index_...]
    all_gather x17 -> x8, waiting for transfers between devices: 681 us -> 35.1 us  [the longest x6 35.1 us: gather_mlp(): lax.all_gather(part, 'dp', axis=0, tiled=True, axis_index_groups=pair_gro...]
    ppermute x4 -> x209, waiting for transfers between devices: 39.6 us -> 473 us  [the longest x201 441 us: swap(): return lax.ppermute(shard, axis, [(i, i ^ bit) for i in range(length)])]
    ppermute x4 -> x209, starting transfers between devices: 9.35 us -> 163 us  [the longest x201 141 us: swap(): return lax.ppermute(shard, axis, [(i, i ^ bit) for i in range(length)])]
    unnamed x320 -> x357, local copies, waits for them, and re-layouts: 16.6 us -> 103 us
    dot_general x21 -> x10, matrix products: 130 us -> 49.7 us  [contract_first(): lax.dot_general(left, right, (((0,), (0,)), ((), ())), preferred_element_...]
    psum x1 -> x0, blocking collectives: 63.4 us -> none  [per_device(): gain_full = lax.psum(gain_total, ('dp', 'tensor'))]
    all_gather x4 -> x0, blocking collectives: 57.6 us -> none  [the longest x1 16.7 us: per_device(): lax.all_gather(value_weight, 'dp', axis=1, tiled=True)]
  transfers between devices with their start and end apart: 40 -> 225, of which waited for: 33 -> 76; matrix products, arithmetic and copies ran while one was open for 12% -> 36% of each run, Pallas kernels for 0% -> 0%
where the time goes in v1:
time: 1160 us
  waiting for transfers between devices  509 us (44%)
  matrix products  191 us (16%)
  starting transfers between devices  165 us (14%)
  local copies, waits for them, and re-layouts  162 us (14%)
  other arithmetic  114 us (10%)
  between operations  17.4 us (1%)
    ppermute x201, waiting for transfers between devices, swap(): return lax.ppermute(shard, axis, [(i, i ^ bit) for i in range(length)])  441 us
    ppermute x201, starting transfers between devices, swap(): return lax.ppermute(shard, axis, [(i, i ^ bit) for i in range(length)])  141 us
    unnamed x357, local copies, waits for them, and re-layouts  103 us
    dot_general x10, matrix products, product(): return jnp.dot(left, right, preferred_element_type=F32)  71.7 us
    dot_general x10, matrix products, contract_first(): lax.dot_general(left, right, (((0,), (0,)), ((), ())), preferred_element_...  49.7 us
    dot_general x10, matrix products, contract_last(): lax.dot_general(left, right, (((1,), (1,)), ((), ())), preferred_element_...  48.3 us
    all_gather x6, waiting for transfers between devices, gather_mlp(): lax.all_gather(part, 'dp', axis=0, tiled=True, axis_index_groups=pair_gro...  35.1 us
    ppermute x4, waiting for transfers between devices, per_device(): got_one = lax.ppermute(one, 'section', [(1, 0)])  31.7 us
  transfers between devices with their start and end apart: 225, of which 76 were waited for; matrix products, arithmetic and copies ran while one was open for 36% of the time, Pallas kernels for 0%

profile of v1, /device:TPU:0, one launch (start us, length us, event | category | flops | bytes accessed | tf_op | source)
XLA Modules:
  0.0 1157.7 jit_solution(18264670249263552485)
XLA Ops:
  13.7 15.2 %collective-permute-done.3 = bf16[528,640]{1,0:T(8,128)(2,1)S(1)} collective-permute-done((bf16[528,640]{1,0:T(8,128)(2,1)S(1)}, bf16[528,640]{1,0:T(8,128)(2,1)S(1)}, u32[]{:S(2)}, u32[]{:S(2)}) %collective-permute-start.3) | collective-permute-done | bytes 675872 | tf_op jit(solution)/shard_map/ppermute | solution.py:16
  39.9 18.3 %collective-permute-done.27 = bf16[512,1024]{1,0:T(8,128)(2,1)} collective-permute-done((bf16[512,1024]{1,0:T(8,128)(2,1)S(1)}, bf16[512,1024]{1,0:T(8,128)(2,1)}, u32[]{:S(2)}, u32[]{:S(2)}) %collective-permute-start.27) | collective-permute-done | bytes 1048608 | tf_op jit(solution)/shard_map/ppermute | solution.py:16
  63.1 34.2 %collective-permute-done.28 = bf16[512,512]{1,0:T(8,128)(2,1)} collective-permute-done((bf16[512,512]{1,0:T(8,128)(2,1)}, bf16[512,512]{1,0:T(8,128)(2,1)}, u32[]{:S(2)}, u32[]{:S(2)}) %collective-permute-start.28) | collective-permute-done | bytes 524320 | tf_op jit(solution)/shard_map/ppermute | solution.py:16
  109.2 17.0 %collective-permute-done.30 = bf16[512,512]{1,0:T(8,128)(2,1)S(1)} collective-permute-done((bf16[512,512]{1,0:T(8,128)(2,1)S(1)}, bf16[512,512]{1,0:T(8,128)(2,1)S(1)}, u32[]{:S(2)}, u32[]{:S(2)}) %collective-permute-start.30) | collective-permute-done | bytes 524320 | tf_op jit(solution)/shard_map/ppermute | solution.py:16
  172.0 19.3 %collective-permute-done.32 = bf16[512,512]{1,0:T(8,128)(2,1)S(1)} collective-permute-done((bf16[512,512]{1,0:T(8,128)(2,1)S(1)}, bf16[512,512]{1,0:T(8,128)(2,1)S(1)}, u32[]{:S(2)}, u32[]{:S(2)}) %collective-permute-start.32) | collective-permute-done | bytes 524320 | tf_op jit(solution)/shard_map/ppermute | solution.py:16
  241.9 7.7 collective-permute-done.14
  269.1 8.5 fusion.156
  277.6 10.3 multiply_convert_fusion.7
  301.4 9.8 collective-permute-done.101
  434.4 8.6 fusion.158
  455.0 8.4 collective-permute-done.68
  463.4 7.7 collective-permute-done.66
  489.8 8.5 fusion.157
  498.3 35.1 %all-gather.17.cloned.1.call-done = bf16[2048,512]{1,0:T(8,128)(2,1)} async-done(((bf16[1024,512]{1,0:T(8,128)(2,1)}), bf16[2048,512]{1,0:T(8,128)(2,1)}) %all-gather.17.cloned.1.call-update) | async-done | bytes 2097168 | tf_op jit(solution)/shard_map/all_gather | solution.py:146
  533.3 11.4 multiply_convert_fusion.5
  633.5 7.8 convolution_convert_fusion.6
  699.8 8.0 collective-permute-done.142
  716.2 8.0 convolution_convert_fusion.10
  724.4 8.3 collective-permute-done.146
  736.7 8.4 collective-permute-done.147
  745.1 7.7 collective-permute-done.145
  771.3 7.8 convolution_convert_fusion.7
  779.2 11.2 multiply_convert_fusion.3
  796.4 10.3 fusion.160
  828.8 9.0 collective-permute-done.168
  860.2 10.3 collective-permute-done.172
  987.6 13.5 %collective-permute-done.205 = bf16[512,512]{1,0:T(8,128)(2,1)} collective-permute-done((bf16[512,512]{1,0:T(8,128)(2,1)}, bf16[512,512]{1,0:T(8,128)(2,1)}, u32[]{:S(2)}, u32[]{:S(2)}) %collective-permute-start.205) | collective-permute-done | bytes 524320 | tf_op jit(solution)/shard_map/ppermute | solution.py:16
  1011.5 39.7 %collective-permute-done.197 = bf16[512,512]{1,0:T(8,128)(2,1)S(1)} collective-permute-done((bf16[512,512]{1,0:T(8,128)(2,1)S(1)}, bf16[512,512]{1,0:T(8,128)(2,1)S(1)}, u32[]{:S(2)}, u32[]{:S(2)}) %collective-permute-start.197) | collective-permute-done | bytes 524320 | tf_op jit(solution)/shard_map/ppermute | solution.py:16
  1071.7 16.1 %collective-permute-done.189 = bf16[96,2048]{1,0:T(8,128)(2,1)S(1)} collective-permute-done((bf16[96,2048]{1,0:T(8,128)(2,1)S(1)}, bf16[96,2048]{1,0:T(8,128)(2,1)S(1)}, u32[]{:S(2)}, u32[]{:S(2)}) %collective-permute-start.189) | collective-permute-done | bytes 393248 | tf_op jit(solution)/shard_map/ppermute | solution.py:16
  1100.8 9.5 collective-permute-done.199
  1112.3 12.0 %collective-permute-done.203 = bf16[512,1024]{1,0:T(8,128)(2,1)} collective-permute-done((bf16[512,1024]{1,0:T(8,128)(2,1)}, bf16[512,1024]{1,0:T(8,128)(2,1)}, u32[]{:S(2)}, u32[]{:S(2)}) %collective-permute-start.203) | collective-permute-done | bytes 1048608 | tf_op jit(solution)/shard_map/ppermute | solution.py:370
  1135.8 10.1 collective-permute-done.195
  (1052 shorter events, 722.8 us)
Async XLA Ops:
  7.2 131.2 %all-gather.23.cloned.1.call-start = ((), (), s32[]{:S(2)}) async-start(), calls=%async_computation.22 | async-start | bytes 3379200 | tf_op jit(solution)/shard_map/all_gather | solution.py:276
  30.3 238.8 %all-gather.11.cloned.1.call-start = ((), (), s32[]{:S(2)}) async-start(), calls=%async_computation.8 | async-start | bytes 3145728 | tf_op jit(solution)/shard_map/all_gather | solution.py:146
  33.9 67.7 %collective-permute-start.1 = (bf16[192,2048]{1,0:T(8,128)(2,1)S(1)}, bf16[192,2048]{1,0:T(8,128)(2,1)}, u32[]{:S(2)}, u32[]{:S(2)}) collective-permute-start(bf16[192,2048]{1,0:T(8,128)(2,1)S(1)} %bitcast.269), channel_id=1, source_target_pairs={{0,2},{1,3},{2,0},{3,1},{4,6},{5,7},{6,4},{7,5},{8,10},{9,11},{10,... | collective-permute-start | bytes 2359304 | tf_op jit(solution)/shard_map/ppermute | solution.py:16
  35.4 70.2 %collective-permute-start = (bf16[192,2048]{1,0:T(8,128)(2,1)S(1)}, bf16[192,2048]{1,0:T(8,128)(2,1)}, u32[]{:S(2)}, u32[]{:S(2)}) collective-permute-start(bf16[192,2048]{1,0:T(8,128)(2,1)S(1)} %bitcast.270), channel_id=1, source_target_pairs={{0,1},{1,0},{2,3},{3,2},{4,5},{5,4},{6,7},{7,6},{8,9},{9,8},{10,11... | collective-permute-start | bytes 2359304 | tf_op jit(solution)/shard_map/ppermute | solution.py:16
  36.6 125.3 %collective-permute-start.31 = (bf16[512,1024]{1,0:T(8,128)(2,1)}, bf16[512,1024]{1,0:T(8,128)(2,1)}, u32[]{:S(2)}, u32[]{:S(2)}) collective-permute-start(bf16[512,1024]{1,0:T(8,128)(2,1)} %slice.867), channel_id=1, source_target_pairs={{0,16},{16,0},{1,17},{17,1},{2,18},{18,2},{3,19},{19,3},{4,20},{20... | collective-permute-start | bytes 3145736 | tf_op jit(solution)/shard_map/ppermute | solution.py:16
  38.1 63.4 %collective-permute-start.29 = (bf16[512,1024]{1,0:T(8,128)(2,1)}, bf16[512,1024]{1,0:T(8,128)(2,1)}, u32[]{:S(2)}, u32[]{:S(2)}) collective-permute-start(bf16[512,1024]{1,0:T(8,128)(2,1)} %slice.865), channel_id=1, source_target_pairs={{0,16},{16,0},{1,17},{17,1},{2,18},{18,2},{3,19},{19,3},{4,20},{20... | collective-permute-start | bytes 3145736 | tf_op jit(solution)/shard_map/ppermute | solution.py:16
  99.8 177.8 %all-gather.13.cloned.1.call-start = ((), (), s32[]{:S(2)}) async-start(), calls=%async_computation.9 | async-start | bytes 3145728 | tf_op jit(solution)/shard_map/all_gather | solution.py:146
  127.6 160.3 %all-gather.15.cloned.1.call-start = ((), (), s32[]{:S(2)}) async-start(), calls=%async_computation.10 | async-start | bytes 3145728 | tf_op jit(solution)/shard_map/all_gather | solution.py:146
  192.8 149.8 %all-gather.25.cloned.1.call-start = ((), (), s32[]{:S(2)}) async-start(), calls=%async_computation.23 | async-start | bytes 3379200 | tf_op jit(solution)/shard_map/all_gather | solution.py:276
  207.7 87.8 %collective-permute-start.99 = (bf16[96,2048]{1,0:T(8,128)(2,1)}, bf16[96,2048]{1,0:T(8,128)(2,1)}, u32[]{:S(2)}, u32[]{:S(2)}) collective-permute-start(bf16[96,2048]{1,0:T(8,128)(2,1)} %get-tuple-element.210), channel_id=1, source_target_pairs={{0,2},{1,3},{2,0},{3,1},{4,6},{5,7},{6,4},{7,5},{8,10},{9,11},{10,... | collective-permute-start | bytes 1179656 | tf_op jit(solution)/shard_map/ppermute | solution.py:16
  208.9 104.6 %collective-permute-start.102 = (bf16[96,2048]{1,0:T(8,128)(2,1)}, bf16[96,2048]{1,0:T(8,128)(2,1)}, u32[]{:S(2)}, u32[]{:S(2)}) collective-permute-start(bf16[96,2048]{1,0:T(8,128)(2,1)} %collective-permute-done.100), channel_id=1, source_target_pairs={{0,16},{16,0},{1,17},{17,1},{2,18},{18,2},{3,19},{19,3},{4,20},{20... | collective-permute-start | bytes 1179656 | tf_op jit(solution)/shard_map/ppermute | solution.py:16
  222.3 212.1 %all-gather.21.cloned.1.call-start = ((), (), s32[]{:S(2)}) async-start(), calls=%async_computation.13 | async-start | bytes 3145728 | tf_op jit(solution)/shard_map/all_gather | solution.py:146
  363.1 126.6 %all-gather.19.cloned.1.call-start = ((), (), s32[]{:S(2)}) async-start(), calls=%async_computation.12 | async-start | bytes 3145728 | tf_op jit(solution)/shard_map/all_gather | solution.py:146
  400.5 132.9 %all-gather.17.cloned.1.call-start = ((), (), s32[]{:S(2)}) async-start(), calls=%async_computation.11 | async-start | bytes 3145728 | tf_op jit(solution)/shard_map/all_gather | solution.py:146
  427.6 495.4 %reduce-scatter.23.cloned.1.call-start = ((), (), s32[]{:S(2)}) async-start(), calls=%async_computation.21 | async-start | bytes 3145728 | tf_op jit(solution)/shard_map/reduce_scatter | solution.py:151
  564.2 60.3 %collective-permute-start.82 = (bf16[96,2048]{1,0:T(8,128)(2,1)S(1)}, bf16[96,2048]{1,0:T(8,128)(2,1)S(1)}, u32[]{:S(2)}, u32[]{:S(2)}) collective-permute-start(bf16[96,2048]{1,0:T(8,128)(2,1)S(1)} %get-tuple-element.107), channel_id=1, source_target_pairs={{0,1},{1,0},{2,3},{3,2},{4,5},{5,4},{6,7},{7,6},{8,9},{9,8},{10,11... | collective-permute-start | bytes 1179656 | tf_op jit(solution)/shard_map/ppermute | solution.py:16
  641.3 284.0 %reduce-scatter.19.cloned.1.call-start = ((), (), s32[]{:S(2)}) async-start(), calls=%async_computation.19 | async-start | bytes 3145728 | tf_op jit(solution)/shard_map/reduce_scatter | solution.py:151
  687.2 240.3 %reduce-scatter.15.cloned.1.call-start = ((), (), s32[]{:S(2)}) async-start(), calls=%async_computation.17 | async-start | bytes 3145728 | tf_op jit(solution)/shard_map/reduce_scatter | solution.py:151
  724.2 250.2 %reduce-scatter.21.cloned.1.call-start = ((), (), s32[]{:S(2)}) async-start(), calls=%async_computation.20 | async-start | bytes 3145728 | tf_op jit(solution)/shard_map/reduce_scatter | solution.py:151
  779.1 203.2 %reduce-scatter.17.cloned.1.call-start = ((), (), s32[]{:S(2)}) async-start(), calls=%async_computation.18 | async-start | bytes 3145728 | tf_op jit(solution)/shard_map/reduce_scatter | solution.py:151
  796.2 188.3 %reduce-scatter.13.cloned.1.call-start = ((), (), s32[]{:S(2)}) async-start(), calls=%async_computation.16 | async-start | bytes 3145728 | tf_op jit(solution)/shard_map/reduce_scatter | solution.py:151
  822.6 270.4 %reduce-scatter.11.cloned.1.call-start = ((), (), s32[]{:S(2)}) async-start(), calls=%async_computation.15 | async-start | bytes 3276800 | tf_op jit(solution)/shard_map/reduce_scatter | solution.py:353
  879.6 253.7 %reduce-scatter.9.cloned.1.call-start = ((), (), s32[]{:S(2)}) async-start(), calls=%async_computation.14 | async-start | bytes 3276800 | tf_op jit(solution)/shard_map/reduce_scatter | solution.py:353
  879.6 125.0 %collective-permute-start.97 = (bf16[96,2048]{1,0:T(8,128)(2,1)}, bf16[96,2048]{1,0:T(8,128)(2,1)}, u32[]{:S(2)}, u32[]{:S(2)}) collective-permute-start(bf16[96,2048]{1,0:T(8,128)(2,1)} %get-tuple-element.234), channel_id=1, source_target_pairs={{0,16},{16,0},{1,17},{17,1},{2,18},{18,2},{3,19},{19,3},{4,20},{20... | collective-permute-start | bytes 1179656 | tf_op jit(solution)/shard_map/ppermute | solution.py:16
  925.3 60.5 %collective-permute-start.206 = (bf16[512,512]{1,0:T(8,128)(2,1)}, bf16[512,512]{1,0:T(8,128)(2,1)}, u32[]{:S(2)}, u32[]{:S(2)}) collective-permute-start(bf16[512,512]{1,0:T(8,128)(2,1)} %get-tuple-element.177), channel_id=1, source_target_pairs={{0,4},{4,0},{8,12},{12,8},{1,5},{5,1},{9,13},{13,9},{2,6},{6,2},{1... | collective-permute-start | bytes 1572872 | tf_op jit(solution)/shard_map/ppermute | solution.py:16
  946.6 64.8 %collective-permute-start.198 = (bf16[512,512]{1,0:T(8,128)(2,1)}, bf16[512,512]{1,0:T(8,128)(2,1)}, u32[]{:S(2)}, u32[]{:S(2)}) collective-permute-start(bf16[512,512]{1,0:T(8,128)(2,1)} %get-tuple-element.185), channel_id=1, source_target_pairs={{0,4},{4,0},{8,12},{12,8},{1,5},{5,1},{9,13},{13,9},{2,6},{6,2},{1... | collective-permute-start | bytes 1572872 | tf_op jit(solution)/shard_map/ppermute | solution.py:16
  979.5 76.4 %collective-permute-start.202 = (bf16[512,512]{1,0:T(8,128)(2,1)}, bf16[512,512]{1,0:T(8,128)(2,1)}, u32[]{:S(2)}, u32[]{:S(2)}) collective-permute-start(bf16[512,512]{1,0:T(8,128)(2,1)} %get-tuple-element.181), channel_id=1, source_target_pairs={{0,4},{4,0},{8,12},{12,8},{1,5},{5,1},{9,13},{13,9},{2,6},{6,2},{1... | collective-permute-start | bytes 1572872 | tf_op jit(solution)/shard_map/ppermute | solution.py:16
  1001.1 50.0 %collective-permute-start.197 = (bf16[512,512]{1,0:T(8,128)(2,1)S(1)}, bf16[512,512]{1,0:T(8,128)(2,1)S(1)}, u32[]{:S(2)}, u32[]{:S(2)}) collective-permute-start(bf16[512,512]{1,0:T(8,128)(2,1)S(1)} %get-tuple-element.183), channel_id=1, source_target_pairs={{0,4},{4,0},{8,12},{12,8},{1,5},{5,1},{9,13},{13,9},{2,6},{6,2},{1... | collective-permute-start | bytes 1572872 | tf_op jit(solution)/shard_map/ppermute | solution.py:16
  1004.7 60.2 %collective-permute-start.201 = (bf16[512,512]{1,0:T(8,128)(2,1)S(1)}, bf16[512,512]{1,0:T(8,128)(2,1)S(1)}, u32[]{:S(2)}, u32[]{:S(2)}) collective-permute-start(bf16[512,512]{1,0:T(8,128)(2,1)S(1)} %copy-done.55), channel_id=1, source_target_pairs={{0,4},{4,0},{8,12},{12,8},{1,5},{5,1},{9,13},{13,9},{2,6},{6,2},{1... | collective-permute-start | bytes 1572872 | tf_op jit(solution)/shard_map/ppermute | solution.py:16
  1006.7 83.5 %collective-permute-start.208 = (bf16[512,1024]{1,0:T(8,128)(2,1)S(1)}, bf16[512,1024]{1,0:T(8,128)(2,1)}, u32[]{:S(2)}, u32[]{:S(2)}) collective-permute-start(bf16[512,1024]{1,0:T(8,128)(2,1)S(1)} %get-tuple-element.42), channel_id=1, source_target_pairs={{0,16},{1,17},{2,18},{3,19},{4,20},{5,21},{6,22},{7,23},{8,24},{9,... | collective-permute-start | bytes 3145736 | tf_op jit(solution)/shard_map/ppermute | solution.py:371
  1011.4 48.1 %collective-permute-start.194 = (f32[2,512]{1,0:T(2,128)S(1)}, f32[2,512]{1,0:T(2,128)S(1)}, u32[]{:S(2)}, u32[]{:S(2)}) collective-permute-start(f32[2,512]{1,0:T(2,128)S(1)} %add.614), channel_id=1, source_target_pairs={{0,1},{1,0},{2,3},{3,2},{4,5},{5,4},{6,7},{7,6},{8,9},{9,8},{10,11... | collective-permute-start | bytes 12296 | tf_op jit(solution)/shard_map/ppermute | solution.py:16
  1064.8 45.5 %collective-permute-start.199 = (bf16[512,1024]{1,0:T(8,128)(2,1)}, bf16[512,1024]{1,0:T(8,128)(2,1)}, u32[]{:S(2)}, u32[]{:S(2)}) collective-permute-start(bf16[512,1024]{1,0:T(8,128)(2,1)} %get-tuple-element.49), channel_id=1, source_target_pairs={{16,0},{17,1},{18,2},{19,3},{20,4},{21,5},{22,6},{23,7},{24,8},{25... | collective-permute-start | bytes 3145736 | tf_op jit(solution)/shard_map/ppermute | solution.py:370
  (320 other events, 4721.0 us)
Sparse Core Ops, SparseCore 0:
  30.5 67.0 all-gather.22
  99.9 56.5 all-gather.10
  158.7 55.4 all-gather.12
  215.6 55.5 all-gather.14
  272.6 55.1 all-gather.24
  363.2 55.2 all-gather.20
  420.7 55.5 all-gather.18
  477.8 55.5 all-gather.16
  641.4 52.5 reduce-scatter.22
  696.2 54.2 reduce-scatter.18
  752.7 54.2 reduce-scatter.14
  809.1 54.3 reduce-scatter.20
  865.7 54.2 reduce-scatter.16
  922.2 54.6 reduce-scatter.12
  979.0 86.4 reduce-scatter.10
  1067.7 52.1 reduce-scatter.8

commit v2 on v1

--- a/solution.py
+++ b/solution.py
@@ -30,6 +30,10 @@
 
 def over_z(shard):
     return swap(shard, "dp", 1)
+
+
+def after(value, *earlier):
+    return lax.optimization_barrier((value, earlier))[0]
 
 
 def rows_of(parts):
@@ -137,12 +141,15 @@
     )
 
 
-def gather_mlp(part):
+def exchange_mlp(part):
     low = lax.axis_index("dp") & 1
     half = part.shape[1] // 2
     kept = lax.dynamic_slice_in_dim(part, low * half, half, 1)
     sent = lax.dynamic_slice_in_dim(part, (1 - low) * half, half, 1)
-    part = ordered(low, kept, over_z(sent), 0)
+    return ordered(low, kept, over_z(sent), 0)
+
+
+def gather_mlp(part):
     return lax.all_gather(part, "dp", axis=0, tiled=True, axis_index_groups=pair_groups())
 
 
@@ -269,6 +276,7 @@
         got = over_y(weight[:, half:])
         mlp[0].append(jnp.where(first, weight[:, :half], got))
         mlp[1].append(jnp.where(first, got, weight[:, :half]))
+    parts = [[exchange_mlp(part) for part in section_parts] for section_parts in mlp]
     full_attention = []
     full_mlp = []
     gains = []
@@ -279,7 +287,7 @@
         gains.append(
             [whole[:, depth + row, :depth].reshape(features).astype(F32) for row in range(2)]
         )
-        full_mlp.append([gather_mlp(part) for part in mlp[index]])
+        full_mlp.append([gather_mlp(part) for part in parts[index]])
 
     quarter = lax.axis_index("tensor")
     positions = jnp.concatenate(
@@ -308,13 +316,19 @@
             unit_a, inverse_a = normalize(start)
             rows_a = gather_eight((unit_a * gains[index][0]).astype(BF16))
         middle, (mixed, attended) = attention_half(start, rows_a, full_attention[index], tables)
+        if index == 0:
+            out_rows = gather_sixteen(both_out[0], both_out[1])
+        else:
+            middle = after(middle, out_rows)
         unit_b, inverse_b = normalize(middle)
         rows_b = gather_sixteen((unit_b * gains[index][1]).astype(BF16))
         gate = product(rows_b, full_mlp[index][0])
         up = product(rows_b, full_mlp[index][1])
         hidden = (jax.nn.silu(gate) * up).astype(BF16)
-        branch = scatter_sixteen(contract_last(hidden, full_mlp[index][2]).astype(BF16))
-        result = (middle + branch).astype(BF16)
+        part = contract_last(hidden, full_mlp[index][2]).astype(BF16)
+        if index == 0:
+            part = after(part, *parts[1])
+        result = (middle + scatter_sixteen(part)).astype(BF16)
         outputs.append(result)
         start = result.astype(F32)
         saved.append(
@@ -322,7 +336,6 @@
         )
 
     grad = both_out[0].astype(F32)
-    out_rows = gather_sixteen(both_out[0], both_out[1])
     input_grads = [None, None]
     matrix = [None, None]
     gain_grads = [None, None]

time: 1160 us -> 1250 us (1.078)
  waiting for transfers between devices: 509 us -> 580 us
    ppermute x201, waiting for transfers between devices: 441 us -> 498 us  [swap(): return lax.ppermute(shard, axis, [(i, i ^ bit) for i in range(length)])]
    unnamed x357 -> x347, local copies, waits for them, and re-layouts: 103 us -> 98 us
  transfers between devices with their start and end apart: 225 -> 225, of which waited for: 76 -> 85; matrix products, arithmetic and copies ran while one was open for 36% -> 34% of each run, Pallas kernels for 0% -> 0%
where the time goes in v2:
time: 1250 us
  waiting for transfers between devices  580 us (46%)
  matrix products  202 us (16%)
  starting transfers between devices  168 us (13%)
  local copies, waits for them, and re-layouts  158 us (13%)
  other arithmetic  121 us (10%)
  between operations  17 us (1%)
    ppermute x201, waiting for transfers between devices, swap(): return lax.ppermute(shard, axis, [(i, i ^ bit) for i in range(length)])  498 us
    ppermute x201, starting transfers between devices, swap(): return lax.ppermute(shard, axis, [(i, i ^ bit) for i in range(length)])  145 us
    unnamed x347, local copies, waits for them, and re-layouts  98 us
    dot_general x10, matrix products, product(): return jnp.dot(left, right, preferred_element_type=F32)  69.7 us
    dot_general x10, matrix products, contract_last(): lax.dot_general(left, right, (((1,), (1,)), ((), ())), preferred_element_...  59.2 us
    dot_general x10, matrix products, contract_first(): lax.dot_general(left, right, (((0,), (0,)), ((), ())), preferred_element_...  52.4 us
    all_gather x6, waiting for transfers between devices, gather_mlp(): lax.all_gather(part, 'dp', axis=0, tiled=True, axis_index_groups=pair_gro...  42.9 us
    ppermute x4, waiting for transfers between devices, per_device(): got_one = lax.ppermute(one, 'section', [(1, 0)])  36.3 us
  transfers between devices with their start and end apart: 225, of which 85 were waited for; matrix products, arithmetic and copies ran while one was open for 34% of the time, Pallas kernels for 0%

profile of v2, /device:TPU:0, one launch (start us, length us, event | category | flops | bytes accessed | tf_op | source)
XLA Modules:
  0.0 1245.7 jit_solution(8491025077107082468)
XLA Ops:
  15.2 15.5 %collective-permute-done.3 = bf16[528,640]{1,0:T(8,128)(2,1)} collective-permute-done((bf16[528,640]{1,0:T(8,128)(2,1)}, bf16[528,640]{1,0:T(8,128)(2,1)}, u32[]{:S(2)}, u32[]{:S(2)}) %collective-permute-start.3) | collective-permute-done | bytes 675872 | tf_op jit(solution)/shard_map/ppermute | solution.py:16
  36.2 22.9 %collective-permute-done.27 = bf16[512,1024]{1,0:T(8,128)(2,1)} collective-permute-done((bf16[512,1024]{1,0:T(8,128)(2,1)}, bf16[512,1024]{1,0:T(8,128)(2,1)}, u32[]{:S(2)}, u32[]{:S(2)}) %collective-permute-start.27) | collective-permute-done | bytes 1048608 | tf_op jit(solution)/shard_map/ppermute | solution.py:16
  68.6 31.5 %collective-permute-done.28 = bf16[512,512]{1,0:T(8,128)(2,1)} collective-permute-done((bf16[512,512]{1,0:T(8,128)(2,1)}, bf16[512,512]{1,0:T(8,128)(2,1)}, u32[]{:S(2)}, u32[]{:S(2)}) %collective-permute-start.28) | collective-permute-done | bytes 524320 | tf_op jit(solution)/shard_map/ppermute | solution.py:16
  114.4 22.4 %collective-permute-done.30 = bf16[512,512]{1,0:T(8,128)(2,1)} collective-permute-done((bf16[512,512]{1,0:T(8,128)(2,1)}, bf16[512,512]{1,0:T(8,128)(2,1)}, u32[]{:S(2)}, u32[]{:S(2)}) %collective-permute-start.30) | collective-permute-done | bytes 524320 | tf_op jit(solution)/shard_map/ppermute | solution.py:16
  149.7 19.4 %collective-permute-done.32 = bf16[512,512]{1,0:T(8,128)(2,1)S(1)} collective-permute-done((bf16[512,512]{1,0:T(8,128)(2,1)S(1)}, bf16[512,512]{1,0:T(8,128)(2,1)S(1)}, u32[]{:S(2)}, u32[]{:S(2)}) %collective-permute-start.32) | collective-permute-done | bytes 524320 | tf_op jit(solution)/shard_map/ppermute | solution.py:16
  235.8 9.5 collective-permute-done.35
  248.3 19.6 %collective-permute-done.34 = bf16[512,512]{1,0:T(8,128)(2,1)} collective-permute-done((bf16[512,512]{1,0:T(8,128)(2,1)}, bf16[512,512]{1,0:T(8,128)(2,1)}, u32[]{:S(2)}, u32[]{:S(2)}) %collective-permute-start.34) | collective-permute-done | bytes 524320 | tf_op jit(solution)/shard_map/ppermute | solution.py:16
  270.7 11.0 collective-permute-done.33
  285.9 17.7 %collective-permute-done.15 = bf16[96,2048]{1,0:T(8,128)(2,1)S(1)} collective-permute-done((bf16[96,2048]{1,0:T(8,128)(2,1)}, bf16[96,2048]{1,0:T(8,128)(2,1)S(1)}, u32[]{:S(2)}, u32[]{:S(2)}) %collective-permute-start.15) | collective-permute-done | bytes 393248 | tf_op jit(solution)/shard_map/ppermute | solution.py:16
  344.8 8.5 fusion.156
  353.3 10.3 multiply_convert_fusion.7
  363.6 16.5 %convolution_convert_fusion.1 = bf16[1536,2048]{1,0:T(8,128)(2,1)S(1)} fusion(bf16[1536,512]{1,0:T(8,128)(2,1)} %get-tuple-element.268, bf16[2048,512]{1,0:T(8,128)(2,1)} %all-gather.15.cloned.1.call-done), kind=kOutput, calls=%fused_computation.7 | convolution fusion | flops 3224371200 | bytes 9961472 | tf_op jit(solution)/shard_map/dot_general | solution.py:48
  512.2 8.6 fusion.158
  529.0 8.3 collective-permute-done.85
  537.3 8.0 collective-permute-done.83
  564.2 9.2 fusion.157
  573.4 42.9 %all-gather.17.cloned.1.call-done = bf16[2048,512]{1,0:T(8,128)(2,1)} async-done(((bf16[1024,512]{1,0:T(8,128)(2,1)}), bf16[2048,512]{1,0:T(8,128)(2,1)}) %all-gather.17.cloned.1.call-update) | async-done | bytes 2097168 | tf_op jit(solution)/shard_map/all_gather | solution.py:153
  616.3 11.4 multiply_convert_fusion.5
  716.1 7.8 convolution_convert_fusion.6
  781.6 8.3 collective-permute-done.142
  805.9 8.3 collective-permute-done.146
  818.3 8.4 collective-permute-done.147
  861.0 9.3 multiply_convert_fusion.3
  879.2 10.3 fusion.160
  911.7 9.1 collective-permute-done.168
  942.6 10.5 collective-permute-done.172
  1070.0 13.8 %collective-permute-done.205 = bf16[512,512]{1,0:T(8,128)(2,1)} collective-permute-done((bf16[512,512]{1,0:T(8,128)(2,1)}, bf16[512,512]{1,0:T(8,128)(2,1)}, u32[]{:S(2)}, u32[]{:S(2)}) %collective-permute-start.205) | collective-permute-done | bytes 524320 | tf_op jit(solution)/shard_map/ppermute | solution.py:16
  1094.4 39.4 %collective-permute-done.197 = bf16[512,512]{1,0:T(8,128)(2,1)S(1)} collective-permute-done((bf16[512,512]{1,0:T(8,128)(2,1)S(1)}, bf16[512,512]{1,0:T(8,128)(2,1)S(1)}, u32[]{:S(2)}, u32[]{:S(2)}) %collective-permute-start.197) | collective-permute-done | bytes 524320 | tf_op jit(solution)/shard_map/ppermute | solution.py:16
  1155.4 15.0 %collective-permute-done.189 = bf16[96,2048]{1,0:T(8,128)(2,1)S(1)} collective-permute-done((bf16[96,2048]{1,0:T(8,128)(2,1)S(1)}, bf16[96,2048]{1,0:T(8,128)(2,1)S(1)}, u32[]{:S(2)}, u32[]{:S(2)}) %collective-permute-start.189) | collective-permute-done | bytes 393248 | tf_op jit(solution)/shard_map/ppermute | solution.py:16
  1182.7 10.3 collective-permute-done.199
  1196.8 14.2 %collective-permute-done.203 = bf16[512,1024]{1,0:T(8,128)(2,1)} collective-permute-done((bf16[512,1024]{1,0:T(8,128)(2,1)}, bf16[512,1024]{1,0:T(8,128)(2,1)}, u32[]{:S(2)}, u32[]{:S(2)}) %collective-permute-start.203) | collective-permute-done | bytes 1048608 | tf_op jit(solution)/shard_map/ppermute | solution.py:383
  1222.5 11.7 collective-permute-done.195
  (1042 shorter events, 758.9 us)
Async XLA Ops:
  7.2 172.3 %all-gather.23.cloned.1.call-start = ((), (), s32[]{:S(2)}) async-start(), calls=%async_computation.22 | async-start | bytes 3379200 | tf_op jit(solution)/shard_map/all_gather | solution.py:284
  33.3 311.5 %all-gather.11.cloned.1.call-start = ((), (), s32[]{:S(2)}) async-start(), calls=%async_computation.8 | async-start | bytes 3145728 | tf_op jit(solution)/shard_map/all_gather | solution.py:153
  63.5 77.7 %collective-permute-start.1 = (bf16[192,2048]{1,0:T(8,128)(2,1)S(1)}, bf16[192,2048]{1,0:T(8,128)(2,1)}, u32[]{:S(2)}, u32[]{:S(2)}) collective-permute-start(bf16[192,2048]{1,0:T(8,128)(2,1)S(1)} %bitcast.269), channel_id=1, source_target_pairs={{0,2},{1,3},{2,0},{3,1},{4,6},{5,7},{6,4},{7,5},{8,10},{9,11},{10,... | collective-permute-start | bytes 2359304 | tf_op jit(solution)/shard_map/ppermute | solution.py:16
  65.1 81.1 %collective-permute-start = (bf16[192,2048]{1,0:T(8,128)(2,1)S(1)}, bf16[192,2048]{1,0:T(8,128)(2,1)}, u32[]{:S(2)}, u32[]{:S(2)}) collective-permute-start(bf16[192,2048]{1,0:T(8,128)(2,1)S(1)} %bitcast.270), channel_id=1, source_target_pairs={{0,1},{1,0},{2,3},{3,2},{4,5},{5,4},{6,7},{7,6},{8,9},{9,8},{10,11... | collective-permute-start | bytes 2359304 | tf_op jit(solution)/shard_map/ppermute | solution.py:16
  102.7 250.7 %all-gather.13.cloned.1.call-start = ((), (), s32[]{:S(2)}) async-start(), calls=%async_computation.9 | async-start | bytes 3145728 | tf_op jit(solution)/shard_map/all_gather | solution.py:153
  105.1 104.3 %collective-permute-start.67 = (bf16[96,2048]{1,0:T(8,128)(2,1)}, bf16[96,2048]{1,0:T(8,128)(2,1)}, u32[]{:S(2)}, u32[]{:S(2)}) collective-permute-start(bf16[96,2048]{1,0:T(8,128)(2,1)} %get-tuple-element.213), channel_id=1, source_target_pairs={{0,2},{1,3},{2,0},{3,1},{4,6},{5,7},{6,4},{7,5},{8,10},{9,11},{10,... | collective-permute-start | bytes 1179656 | tf_op jit(solution)/shard_map/ppermute | solution.py:16
  139.4 224.2 %all-gather.15.cloned.1.call-start = ((), (), s32[]{:S(2)}) async-start(), calls=%async_computation.10 | async-start | bytes 3145728 | tf_op jit(solution)/shard_map/all_gather | solution.py:153
  170.6 260.0 %all-gather.25.cloned.1.call-start = ((), (), s32[]{:S(2)}) async-start(), calls=%async_computation.23 | async-start | bytes 3379200 | tf_op jit(solution)/shard_map/all_gather | solution.py:284
  211.3 300.9 %all-gather.21.cloned.1.call-start = ((), (), s32[]{:S(2)}) async-start(), calls=%async_computation.13 | async-start | bytes 3145728 | tf_op jit(solution)/shard_map/all_gather | solution.py:153
  225.9 55.9 %collective-permute-start.33 = (bf16[512,512]{1,0:T(8,128)(2,1)}, bf16[512,512]{1,0:T(8,128)(2,1)}, u32[]{:S(2)}, u32[]{:S(2)}) collective-permute-start(bf16[512,512]{1,0:T(8,128)(2,1)} %get-tuple-element.194), channel_id=1, source_target_pairs={{0,4},{4,0},{8,12},{12,8},{1,5},{5,1},{9,13},{13,9},{2,6},{6,2},{1... | collective-permute-start | bytes 1572872 | tf_op jit(solution)/shard_map/ppermute | solution.py:16
  234.3 69.4 %collective-permute-start.15 = (bf16[96,2048]{1,0:T(8,128)(2,1)}, bf16[96,2048]{1,0:T(8,128)(2,1)S(1)}, u32[]{:S(2)}, u32[]{:S(2)}) collective-permute-start(bf16[96,2048]{1,0:T(8,128)(2,1)} %get-tuple-element.73), channel_id=1, source_target_pairs={{0,4},{4,0},{8,12},{12,8},{1,5},{5,1},{9,13},{13,9},{2,6},{6,2},{1... | collective-permute-start | bytes 1179656 | tf_op jit(solution)/shard_map/ppermute | solution.py:16
  234.3 69.4 %collective-permute-start.13 = (bf16[96,2048]{1,0:T(8,128)(2,1)}, bf16[96,2048]{1,0:T(8,128)(2,1)S(1)}, u32[]{:S(2)}, u32[]{:S(2)}) collective-permute-start(bf16[96,2048]{1,0:T(8,128)(2,1)} %get-tuple-element.73), channel_id=1, source_target_pairs={{0,16},{16,0},{1,17},{17,1},{2,18},{18,2},{3,19},{19,3},{4,20},{20... | collective-permute-start | bytes 1179656 | tf_op jit(solution)/shard_map/ppermute | solution.py:16
  245.4 59.9 %collective-permute-start.12 = (bf16[96,2048]{1,0:T(8,128)(2,1)}, bf16[96,2048]{1,0:T(8,128)(2,1)}, u32[]{:S(2)}, u32[]{:S(2)}) collective-permute-start(bf16[96,2048]{1,0:T(8,128)(2,1)} %get-tuple-element.73), channel_id=1, source_target_pairs={{0,2},{1,3},{2,0},{3,1},{4,6},{5,7},{6,4},{7,5},{8,10},{9,11},{10,... | collective-permute-start | bytes 1179656 | tf_op jit(solution)/shard_map/ppermute | solution.py:16
  267.9 115.0 %collective-permute-start.69 = (bf16[96,2048]{1,0:T(8,128)(2,1)}, bf16[96,2048]{1,0:T(8,128)(2,1)}, u32[]{:S(2)}, u32[]{:S(2)}) collective-permute-start(bf16[96,2048]{1,0:T(8,128)(2,1)} %get-tuple-element.213), channel_id=1, source_target_pairs={{0,4},{4,0},{8,12},{12,8},{1,5},{5,1},{9,13},{13,9},{2,6},{6,2},{1... | collective-permute-start | bytes 1179656 | tf_op jit(solution)/shard_map/ppermute | solution.py:16
  281.8 99.4 %collective-permute-start.68 = (bf16[96,2048]{1,0:T(8,128)(2,1)}, bf16[96,2048]{1,0:T(8,128)(2,1)}, u32[]{:S(2)}, u32[]{:S(2)}) collective-permute-start(bf16[96,2048]{1,0:T(8,128)(2,1)} %get-tuple-element.212), channel_id=1, source_target_pairs={{0,2},{1,3},{2,0},{3,1},{4,6},{5,7},{6,4},{7,5},{8,10},{9,11},{10,... | collective-permute-start | bytes 1179656 | tf_op jit(solution)/shard_map/ppermute | solution.py:16
  446.9 117.3 %all-gather.19.cloned.1.call-start = ((), (), s32[]{:S(2)}) async-start(), calls=%async_computation.12 | async-start | bytes 3145728 | tf_op jit(solution)/shard_map/all_gather | solution.py:153
  481.9 134.3 %all-gather.17.cloned.1.call-start = ((), (), s32[]{:S(2)}) async-start(), calls=%async_computation.11 | async-start | bytes 3145728 | tf_op jit(solution)/shard_map/all_gather | solution.py:153
  497.8 507.9 %reduce-scatter.23.cloned.1.call-start = ((), (), s32[]{:S(2)}) async-start(), calls=%async_computation.21 | async-start | bytes 3145728 | tf_op jit(solution)/shard_map/reduce_scatter | solution.py:158
  646.9 60.3 %collective-permute-start.96 = (bf16[96,2048]{1,0:T(8,128)(2,1)S(1)}, bf16[96,2048]{1,0:T(8,128)(2,1)S(1)}, u32[]{:S(2)}, u32[]{:S(2)}) collective-permute-start(bf16[96,2048]{1,0:T(8,128)(2,1)S(1)} %get-tuple-element.109), channel_id=1, source_target_pairs={{0,1},{1,0},{2,3},{3,2},{4,5},{5,4},{6,7},{7,6},{8,9},{9,8},{10,11... | collective-permute-start | bytes 1179656 | tf_op jit(solution)/shard_map/ppermute | solution.py:16
  723.9 284.1 %reduce-scatter.19.cloned.1.call-start = ((), (), s32[]{:S(2)}) async-start(), calls=%async_computation.19 | async-start | bytes 3145728 | tf_op jit(solution)/shard_map/reduce_scatter | solution.py:158
  768.5 241.7 %reduce-scatter.15.cloned.1.call-start = ((), (), s32[]{:S(2)}) async-start(), calls=%async_computation.17 | async-start | bytes 3145728 | tf_op jit(solution)/shard_map/reduce_scatter | solution.py:158
  805.7 251.5 %reduce-scatter.21.cloned.1.call-start = ((), (), s32[]{:S(2)}) async-start(), calls=%async_computation.20 | async-start | bytes 3145728 | tf_op jit(solution)/shard_map/reduce_scatter | solution.py:158
  860.7 204.2 %reduce-scatter.17.cloned.1.call-start = ((), (), s32[]{:S(2)}) async-start(), calls=%async_computation.18 | async-start | bytes 3145728 | tf_op jit(solution)/shard_map/reduce_scatter | solution.py:158
  879.2 187.9 %reduce-scatter.13.cloned.1.call-start = ((), (), s32[]{:S(2)}) async-start(), calls=%async_computation.16 | async-start | bytes 3145728 | tf_op jit(solution)/shard_map/reduce_scatter | solution.py:158
  905.4 270.4 %reduce-scatter.11.cloned.1.call-start = ((), (), s32[]{:S(2)}) async-start(), calls=%async_computation.15 | async-start | bytes 3276800 | tf_op jit(solution)/shard_map/reduce_scatter | solution.py:366
  962.3 257.7 %reduce-scatter.9.cloned.1.call-start = ((), (), s32[]{:S(2)}) async-start(), calls=%async_computation.14 | async-start | bytes 3276800 | tf_op jit(solution)/shard_map/reduce_scatter | solution.py:366
  962.3 125.3 %collective-permute-start.111 = (bf16[96,2048]{1,0:T(8,128)(2,1)}, bf16[96,2048]{1,0:T(8,128)(2,1)}, u32[]{:S(2)}, u32[]{:S(2)}) collective-permute-start(bf16[96,2048]{1,0:T(8,128)(2,1)} %get-tuple-element.236), channel_id=1, source_target_pairs={{0,16},{16,0},{1,17},{17,1},{2,18},{18,2},{3,19},{19,3},{4,20},{20... | collective-permute-start | bytes 1179656 | tf_op jit(solution)/shard_map/ppermute | solution.py:16
  1008.0 60.3 %collective-permute-start.206 = (bf16[512,512]{1,0:T(8,128)(2,1)}, bf16[512,512]{1,0:T(8,128)(2,1)}, u32[]{:S(2)}, u32[]{:S(2)}) collective-permute-start(bf16[512,512]{1,0:T(8,128)(2,1)} %get-tuple-element.179), channel_id=1, source_target_pairs={{0,4},{4,0},{8,12},{12,8},{1,5},{5,1},{9,13},{13,9},{2,6},{6,2},{1... | collective-permute-start | bytes 1572872 | tf_op jit(solution)/shard_map/ppermute | solution.py:16
  1028.9 65.4 %collective-permute-start.198 = (bf16[512,512]{1,0:T(8,128)(2,1)}, bf16[512,512]{1,0:T(8,128)(2,1)}, u32[]{:S(2)}, u32[]{:S(2)}) collective-permute-start(bf16[512,512]{1,0:T(8,128)(2,1)} %get-tuple-element.187), channel_id=1, source_target_pairs={{0,4},{4,0},{8,12},{12,8},{1,5},{5,1},{9,13},{13,9},{2,6},{6,2},{1... | collective-permute-start | bytes 1572872 | tf_op jit(solution)/shard_map/ppermute | solution.py:16
  1062.2 76.4 %collective-permute-start.202 = (bf16[512,512]{1,0:T(8,128)(2,1)}, bf16[512,512]{1,0:T(8,128)(2,1)}, u32[]{:S(2)}, u32[]{:S(2)}) collective-permute-start(bf16[512,512]{1,0:T(8,128)(2,1)} %get-tuple-element.183), channel_id=1, source_target_pairs={{0,4},{4,0},{8,12},{12,8},{1,5},{5,1},{9,13},{13,9},{2,6},{6,2},{1... | collective-permute-start | bytes 1572872 | tf_op jit(solution)/shard_map/ppermute | solution.py:16
  1087.6 60.9 %collective-permute-start.201 = (bf16[512,512]{1,0:T(8,128)(2,1)S(1)}, bf16[512,512]{1,0:T(8,128)(2,1)S(1)}, u32[]{:S(2)}, u32[]{:S(2)}) collective-permute-start(bf16[512,512]{1,0:T(8,128)(2,1)S(1)} %copy-done.52), channel_id=1, source_target_pairs={{0,4},{4,0},{8,12},{12,8},{1,5},{5,1},{9,13},{13,9},{2,6},{6,2},{1... | collective-permute-start | bytes 1572872 | tf_op jit(solution)/shard_map/ppermute | solution.py:16
  1089.6 83.3 %collective-permute-start.208 = (bf16[512,1024]{1,0:T(8,128)(2,1)S(1)}, bf16[512,1024]{1,0:T(8,128)(2,1)}, u32[]{:S(2)}, u32[]{:S(2)}) collective-permute-start(bf16[512,1024]{1,0:T(8,128)(2,1)S(1)} %get-tuple-element.46), channel_id=1, source_target_pairs={{0,16},{1,17},{2,18},{3,19},{4,20},{5,21},{6,22},{7,23},{8,24},{9,... | collective-permute-start | bytes 3145736 | tf_op jit(solution)/shard_map/ppermute | solution.py:384
  (315 other events, 5009.5 us)
Sparse Core Ops, SparseCore 0:
  33.4 67.0 all-gather.22
  102.8 56.7 all-gather.10
  161.7 55.5 all-gather.12
  218.7 54.5 all-gather.14
  274.7 65.3 all-gather.24
  447.0 55.0 all-gather.20
  503.6 55.5 all-gather.18
  560.7 55.4 all-gather.16
  724.1 52.5 reduce-scatter.22
  778.8 54.2 reduce-scatter.18
  835.3 54.2 reduce-scatter.14
  891.8 54.3 reduce-scatter.20
  948.4 54.2 reduce-scatter.16
  1004.9 54.6 reduce-scatter.12
  1061.7 87.0 reduce-scatter.10
  1150.9 52.6 reduce-scatter.8
